TPU v7x, 256 devices: a whole 4x4x8 slice. The times are simulated.
256 devices in a mesh: mom: 8 (over z_lo, x), pts: 32 (over y, z_hi, core).
Axes of the slice: x: 4, y: 4, z: 8 (z_hi: 4, z_lo: 2; z = z_hi * 2 + z_lo), core: 2. Of those that a mesh axis runs over, the one named last changes fastest.
Arguments:
- amplitudes: bfloat16 [2, 2, 1, 256, 64, 128], P(None, None, None, 'mom'), may hold values from -6 to 6
- val_orbitals: bfloat16 [2, 256, 64, 512], P(None, 'mom'), may hold values from -0.25 to 0.25
- cond_orbitals: bfloat16 [2, 256, 512, 128], P(None, 'mom', 'pts'), may hold values from -0.25 to 0.25
- screened: bfloat16 [2, 256, 512, 512], P(None, None, ('pts', 'mom')), may hold values from -12 to 12
- val_energy: float32 [256, 64], P('mom', 'pts'), may hold values from -2 to -0.5
- cond_energy: float32 [256, 128], P('mom'), may hold values from 0.5 to 2
- grid_of_slot: int32 [256], replicated, may hold values from 0 to 255, as said below
- opposite_slot: int32 [256], P('mom'), may hold values from 0 to 255, as said below
Outputs:
- applied: float32 [2, 2, 1, 256, 64, 128], P(None, None, None, 'mom', 'pts')
Inputs may be any that keep to these rules, and one draw needn't show every extreme that they name: `grid_of_slot`: a permutation of the grid indices. opposite_slot[s] is the slot whose grid index is 255 - grid_of_slot[s]; it is never s, and s and opposite_slot[s] lie in aligned blocks of 32 slots whose first slots differ by 128.
All inputs are finite; a program needn't handle non-finite values.
Results may differ from a plain program's by a relative error of at most 0.006.
Values may be sent and summed in bfloat16 or wider, within the bound.
A program may use at most 128 MiB of HBM per device.

v0:
```python
import math

import jax
import jax.numpy as jnp
from jax import lax
from jax.sharding import PartitionSpec as P


def partner_2(value, axis, apart):
    mask = 2**apart
    pairs = [(source, source ^ mask) for source in range(lax.axis_size(axis))]
    return lax.ppermute(value, axis, pairs)


def complex_mix(formula, left, right, left_sign, right_sign):
    real_real = jnp.einsum(formula, left[0], right[0], preferred_element_type=jnp.float32)
    imag_imag = jnp.einsum(formula, left[1], right[1], preferred_element_type=jnp.float32)
    real_imag = jnp.einsum(formula, left[0], right[1], preferred_element_type=jnp.float32)
    imag_real = jnp.einsum(formula, left[1], right[0], preferred_element_type=jnp.float32)
    return jnp.stack(
        [
            real_real - left_sign * right_sign * imag_imag,
            right_sign * real_imag + left_sign * imag_real,
        ]
    )


def on_device(
    amplitudes,
    val_orbitals,
    cond_orbitals,
    screened,
    val_energy,
    cond_energy,
    grid_of_slot,
    opposite_slot,
):
    slots_here = opposite_slot.shape[0]
    total_slots = grid_of_slot.shape[0]
    rows_here = val_energy.shape[1]
    frequency = jnp.arange(total_slots, dtype=jnp.int32)
    phases = frequency[:, None] * grid_of_slot[None, :] % total_slots
    angles = phases.astype(jnp.float32) * (2.0 * math.pi / total_slots)
    cosine_table = jnp.cos(angles).astype(jnp.bfloat16)
    sine_table = jnp.sin(angles).astype(jnp.bfloat16)
    half_product = complex_mix("bnkvc,kuc->bnkvu", amplitudes, cond_orbitals, 1.0, 1.0).astype(
        jnp.bfloat16
    )
    pair_values = complex_mix("bnkvu,kvm->bnkum", half_product, val_orbitals, 1.0, -1.0).astype(
        jnp.bfloat16
    )
    flattened = pair_values.reshape(pair_values.shape[:4] + (-1,))
    weights = screened.reshape(2, total_slots, -1)
    inverse_count = 1.0 / total_slots
    whole_k = lax.all_to_all(flattened, "mom", split_axis=4, concat_axis=3, tiled=True)
    spec_real = jnp.einsum(
        "fs,bnsc->bnfc", cosine_table, whole_k[0], preferred_element_type=jnp.float32
    ) + jnp.einsum("fs,bnsc->bnfc", sine_table, whole_k[1], preferred_element_type=jnp.float32)
    spec_imag = jnp.einsum(
        "fs,bnsc->bnfc", cosine_table, whole_k[1], preferred_element_type=jnp.float32
    ) - jnp.einsum("fs,bnsc->bnfc", sine_table, whole_k[0], preferred_element_type=jnp.float32)
    prod_real = (weights[0] * spec_real - weights[1] * spec_imag).astype(jnp.bfloat16)
    prod_imag = (weights[0] * spec_imag + weights[1] * spec_real).astype(jnp.bfloat16)
    back_real = (
        jnp.einsum("fs,bnfc->bnsc", cosine_table, prod_real, preferred_element_type=jnp.float32)
        - jnp.einsum("fs,bnfc->bnsc", sine_table, prod_imag, preferred_element_type=jnp.float32)
    ) * inverse_count
    back_imag = (
        jnp.einsum("fs,bnfc->bnsc", cosine_table, prod_imag, preferred_element_type=jnp.float32)
        + jnp.einsum("fs,bnfc->bnsc", sine_table, prod_real, preferred_element_type=jnp.float32)
    ) * inverse_count
    field_pts = lax.all_to_all(
        jnp.stack([back_real, back_imag]).astype(jnp.bfloat16),
        "mom",
        split_axis=3,
        concat_axis=4,
        tiled=True,
    )
    field_pts = field_pts.reshape(pair_values.shape)
    weighted = complex_mix("bnkum,kvm->bnkvu", field_pts, val_orbitals, 1.0, 1.0).astype(
        jnp.bfloat16
    )
    band_terms = complex_mix("bnkvu,kuc->bnkvc", weighted, cond_orbitals, 1.0, -1.0)
    band_values = lax.psum_scatter(band_terms, "pts", scatter_dimension=4, tiled=True)
    top_bit = lax.axis_size("mom").bit_length() - 2
    partner = partner_2(band_values.astype(jnp.bfloat16), "mom", top_bit).astype(band_values.dtype)
    mirrored = jnp.take(partner, opposite_slot % slots_here, axis=3)
    start_row = lax.axis_index("pts") * rows_here
    own_rows = lax.dynamic_slice_in_dim(amplitudes, start_row, rows_here, 4).astype(jnp.float32)
    energy_gap = cond_energy[:, None, :] - val_energy[:, :, None]
    result_real = energy_gap * own_rows[0, 0] - band_values[0, 0] - mirrored[0, 1]
    result_imag = energy_gap * own_rows[1, 0] - band_values[1, 0] + mirrored[1, 1]
    anti_real = -energy_gap * own_rows[0, 1] + band_values[0, 1] + mirrored[0, 0]
    anti_imag = -energy_gap * own_rows[1, 1] + band_values[1, 1] - mirrored[1, 0]
    return jnp.stack([jnp.stack([result_real, anti_real]), jnp.stack([result_imag, anti_imag])])


def solution(mesh):
    in_specs = (
        P(None, None, None, "mom", None, None),
        P(None, "mom", None, None),
        P(None, "mom", "pts", None),
        P(None, None, ("pts", "mom"), None),
        P("mom", "pts"),
        P("mom", None),
        P(),
        P("mom"),
    )
    out_specs = P(None, None, None, "mom", "pts", None)
    return jax.shard_map(
        on_device, mesh=mesh, in_specs=in_specs, out_specs=out_specs, check_vma=False
    )
```

profile of v0, /device:TPU:1, one launch (start us, length us, event | category | flops | bytes accessed | tf_op | source)
XLA Modules:
  0.0 284.5 jit_solution(13320353008249521485)
XLA Ops:
  6.5 1.8 fusion.151
  13.4 4.9 %copy.167 = bf16[2,1,32,16,512]{2,0,4,3,1:T(2,128)(2,1)} copy(bf16[2,1,32,16,512]{4,3,0,2,1:T(8,128)(2,1)S(1)} %fusion.24) | data formatting | bytes 2097152 | tf_op jit(solution)/shard_map/stack | solution.py:20
  18.3 2.1 fusion.27
  20.4 4.9 %copy.168 = bf16[2,1,32,16,512]{2,0,4,3,1:T(2,128)(2,1)} copy(bf16[2,1,32,16,512]{4,3,0,2,1:T(8,128)(2,1)S(1)} %fusion.27) | data formatting | bytes 2097152 | tf_op jit(solution)/shard_map/stack | solution.py:20
  25.3 16.3 %fusion.153 = bf16[8192,1,2,2,32]{4,3,2,1,0:T(2,128)(2,1)} fusion(bf16[1,2,1,32,8192]{3,1,0,2,4:T(2,128)(2,1)} %bitcast.313, bf16[1,2,1,32,8192]{3,1,0,2,4:T(2,128)(2,1)} %bitcast.312), kind=kLoop, calls=%fused_computation.180 | loop fusion | flops 1048576 | bytes 4194304
  41.6 11.2 %reshape.527 = bf16[8,2,65536]{2,1,0:T(2,128)(2,1)} reshape(bf16[8192,1,2,2,32]{4,3,2,1,0:T(2,128)(2,1)} %fusion.153) | data formatting | bytes 4194304
  52.9 6.3 %all-to-all-start = ((bf16[8,2,65536]{2,1,0:T(2,128)(2,1)}), bf16[8,2,65536]{2,1,0:T(2,128)(2,1)S(1)}, u32[]{:S(2)}, u32[]{:S(2)}) async-start(bf16[8,2,65536]{2,1,0:T(2,128)(2,1)} %reshape.527), calls=%async_computation | async-start | bytes 4194304 | tf_op jit(solution)/shard_map/all_to_all | solution.py:55
  59.4 2.1 slice_convert_fusion.1
  61.5 1.5 copy.166
  62.9 2.3 copy.170
  65.2 20.1 %all-to-all-done = bf16[8,2,65536]{2,1,0:T(2,128)(2,1)S(1)} async-done(((bf16[8,2,65536]{2,1,0:T(2,128)(2,1)}), bf16[8,2,65536]{2,1,0:T(2,128)(2,1)S(1)}, u32[]{:S(2)}, u32[]{:S(2)}) %all-to-all-start) | async-done | bytes 2097184 | tf_op jit(solution)/shard_map/all_to_all | solution.py:55
  85.3 6.5 %reshape.528 = bf16[8192,1,2,2,32]{4,3,2,1,0:T(2,128)(2,1)} reshape(bf16[8,2,65536]{2,1,0:T(2,128)(2,1)S(1)} %all-to-all-done) | data formatting | bytes 4194304
  91.9 11.9 %copy.169 = bf16[2,2,1,32,8,1024]{5,4,3,1,0,2:T(8,128)(2,1)S(1)} copy(bf16[2,2,1,32,8,1024]{3,1,0,5,4,2:T(2,128)(2,1)} %bitcast.311) | data formatting | bytes 4194304 | tf_op jit(solution)/shard_map/all_to_all | solution.py:55
  105.1 1.4 fusion.92
  106.6 1.4 fusion.94
  108.0 1.4 convolution_subtract_fusion
  109.4 2.5 fusion.63
  111.9 1.4 fusion.90
  113.3 1.4 fusion.88
  114.6 1.4 fusion.30
  116.0 1.4 fusion.31
  117.6 4.1 %copy.142 = bf16[2,2,1,256,1024]{4,1,2,0,3:T(2,128)(2,1)} copy(bf16[2,2,1,256,1024]{3,4,1,2,0:T(8,128)(2,1)S(1)} %pad_maximum_fusion.2) | data formatting | bytes 4194304 | tf_op jit(solution)/shard_map/stack | solution.py:73
  121.7 29.4 %all_to_all.30 = bf16[2,2,1,256,1024]{4,1,2,0,3:T(2,128)(2,1)S(1)} all-to-all(bf16[2,2,1,256,1024]{4,1,2,0,3:T(2,128)(2,1)} %copy.142), channel_id=1, replica_groups=mesh['mom'=8,'pts'=32] {'mom'}, dimensions={3} | all-to-all | bytes 4194304 | tf_op jit(solution)/shard_map/all_to_all | solution.py:72
  151.8 1.2 fusion.149
  154.0 3.2 %fusion.4 = f32[32,2,16,64]{3,2,1,0:T(8,128)} fusion(bf16[2,32,16,512]{3,2,0,1:T(8,128)(2,1)S(1)} %reshape.505, bf16[2,32,64,512]{3,2,1,0:T(8,128)(2,1)} %param.9), kind=kOutput, calls=%fused_computation.12 | convolution fusion | flops 67108864 | bytes 3407872 | tf_op jit(solution)/shard_map/bnkum,kvm->bnkvu/dot_general | solution.py:19
  158.1 2.3 fusion.6
  160.4 2.3 fusion.56
  163.7 1.2 copy-done.1
  167.2 4.4 %copy.146 = f32[2,2,1,32,64,128]{5,3,2,1,0,4:T(8,128)} copy(f32[2,2,1,32,64,128]{5,4,1,3,2,0:T(8,128)S(1)} %pad_maximum_fusion.1) | data formatting | bytes 8388608 | tf_op jit(solution)/shard_map/stack | solution.py:20
  172.4 1.0 dynamic-slice_convert_fusion
  173.4 98.0 %reduce-scatter.2.cloned.1.call-done = f32[2,2,1,32,2,128]{5,3,2,1,0,4:T(8,128)} async-done(((f32[2,2,1,32,64,128]{5,3,2,1,0,4:T(8,128)}), f32[2,2,1,32,2,128]{5,3,2,1,0,4:T(8,128)}) %reduce-scatter.2.cloned.1.call-update) | async-done | bytes 131088 | tf_op jit(solution)/shard_map/reduce_scatter | solution.py:84
  273.7 1.9 collective-permute-done
  (61 shorter events, 17.7 us)
Async XLA Ops:
  6.5 1.8 copy-start.4
  9.2 2.8 copy-start
  11.1 1.4 copy-start.5
  52.9 6.6 %copy-start.7 = (bf16[2,256,2,512]{3,2,1,0:T(2,128)(2,1)S(1)}, bf16[2,256,2,512]{3,2,1,0:T(2,128)(2,1)}, u32[]{:S(2)}) copy-start(bf16[2,256,2,512]{3,2,1,0:T(2,128)(2,1)} %param.11) | copy-start | bytes 3145732
  52.9 32.5 %all-to-all-start = ((bf16[8,2,65536]{2,1,0:T(2,128)(2,1)}), bf16[8,2,65536]{2,1,0:T(2,128)(2,1)S(1)}, u32[]{:S(2)}, u32[]{:S(2)}) async-start(bf16[8,2,65536]{2,1,0:T(2,128)(2,1)} %reshape.527), calls=%async_computation | async-start | bytes 4194304 | tf_op jit(solution)/shard_map/all_to_all | solution.py:55
  59.2 212.2 %reduce-scatter.2.cloned.1.call-start = ((), (), s32[]{:S(2)}) async-start(), calls=%async_computation.3 | async-start | bytes 4325376 | tf_op jit(solution)/shard_map/reduce_scatter | solution.py:84
  104.0 1.2 copy-start.9
  108.0 1.4 copy-start.2
  154.0 3.2 %copy-start.3 = (bf16[1,2,1,32,8,1024]{5,3,4,1,0,2:T(8,128)(2,1)S(1)}, bf16[1,2,1,32,8,1024]{5,3,4,1,0,2:T(8,128)(2,1)}, u32[]{:S(2)}) copy-start(bf16[1,2,1,32,8,1024]{5,3,4,1,0,2:T(8,128)(2,1)} %get-tuple-element.10) | copy-start | bytes 3145732
  162.7 2.2 copy-start.1
  162.7 2.3 copy-start.6
  171.6 0.7 copy-start.10
  171.6 0.8 copy-start.11
  171.6 105.0 %copy-start.8 = (f32[32,128]{1,0:T(8,128)S(1)}, f32[32,128]{1,0:T(8,128)}, u32[]{:S(2)}) copy-start(f32[32,128]{1,0:T(8,128)} %param.13) | copy-start | bytes 49156
  272.4 3.2 %collective-permute-start = (bf16[2,2,1,32,2,128]{5,4,3,1,0,2:T(2,128)(2,1)S(1)}, bf16[2,2,1,32,2,128]{5,4,3,1,0,2:T(2,128)(2,1)S(1)}, u32[]{:S(2)}, u32[]{:S(2)}) collective-permute-start(bf16[2,2,1,32,2,128]{5,4,3,1,0,2:T(2,128)(2,1)S(1)} %copy.199), channel_id=1, source_target_pairs={{0,128},{32,160},{64,192},{96,224},{128,0},{160,32},{192,64},{224,... | collective-permute-start | bytes 196616 | tf_op jit(solution)/shard_map/ppermute | solution.py:12
Sparse Core Ops, SparseCore 0:
  171.7 99.6 reduce-scatter.1
where the time goes:
time: 288 us; the launch traced here: 284 us
  waiting for transfers between devices  120 us (42%)
  local copies, waits for them, and re-layouts  63.2 us (22%)
  matrix products  29.7 us (10%)
  blocking collectives  29.4 us (10%)
  other arithmetic  21.4 us (7%)
  between operations  13.7 us (5%)
  starting transfers between devices  7.02 us (2%)
    reduce_scatter x1, waiting for transfers between devices, on_device(): lax.psum_scatter(band_terms, 'pts', scatter_dimension=4, tiled=True)  98 us
    all_to_all x1, blocking collectives, on_device(): lax.all_to_all(jnp.stack([back_real, back_imag]).astype(jnp.bfloat16), 'm...  29.4 us
    all_to_all x1, waiting for transfers between devices, on_device(): lax.all_to_all(flattened, 'mom', split_axis=4, concat_axis=3, tiled=True)  20.1 us
    unnamed x27, local copies, waits for them, and re-layouts  19.8 us
    unnamed x1, other arithmetic  16.3 us
    another operation x3, local copies, waits for them, and re-layouts, complex_mix(): jnp.stack([real_real - left_sign * right_sign * imag_imag, right_sign * r...  14.2 us
    all_to_all x1, local copies, waits for them, and re-layouts, on_device(): lax.all_to_all(flattened, 'mom', split_axis=4, concat_axis=3, tiled=True)  11.9 us
    all_to_all x1, starting transfers between devices, on_device(): lax.all_to_all(flattened, 'mom', split_axis=4, concat_axis=3, tiled=True)  6.33 us
  transfers between devices with their start and end apart: 3, of which 3 were waited for; matrix products, arithmetic and copies ran while one was open for 3% of the time, Pallas kernels for 0%

commit v1 on v0

v1 whole, which is shorter than its diff:
```python
import math

import jax
import jax.numpy as jnp
from jax import lax
from jax.experimental import pallas as pl
from jax.experimental.pallas import tpu as pltpu
from jax.sharding import PartitionSpec as P

MESH = pl.DeviceIdType.MESH
F32 = jnp.float32
BF16 = jnp.bfloat16
NT = (((1,), (1,)), ((), ()))
TN = (((0,), (0,)), ((), ()))
STEP_A = 4
STEP_D = 4


def dot(a, b, dims=(((1,), (0,)), ((), ()))):
    return lax.dot_general(a, b, dims, preferred_element_type=F32)


def kernel(
    x_hbm, v_hbm, c_hbm, w_hbm, val_e, cond_e, grid_row, opp_row,
    out,
    x, v, c, w, fwd, inv, spread, send1, recv1, send2, recv2, band, own_x,
    send_c, recv_c, own_y, send_y, recv_y, own_z, send_z, recv_z, total, send_p, recv_p,
    load_sem, self_sem, s1, r1, s2, r2, sc, rc, sy, ry, sz, rz, sp, rp,
):
    m = lax.axis_index("mom")
    p = lax.axis_index("pts")
    mx, mz = m % 4, m // 4
    py, ph, pc = p // 8, (p // 2) % 4, p % 2

    def mom_to(j):
        return ((mz + j // 4) % 2) * 4 + (mx + j % 4) % 4

    def mom_from(j):
        return ((mz + j // 4) % 2) * 4 + (mx + 4 - j % 4) % 4

    core_peer = (m, p + 1 - 2 * pc)

    def y_to(d):
        return (m, ((py + d) % 4) * 8 + p % 8)

    def z_to(d):
        return (m, py * 8 + ((ph + d) % 4) * 2 + pc)

    swap_peer = ((m + 4) % 8, p)

    barrier = pltpu.get_barrier_semaphore()
    peers = [(mom_to(j), p) for j in range(1, 8)] + [core_peer]
    peers += [y_to(d) for d in range(1, 4)] + [z_to(d) for d in range(1, 4)]
    for peer in peers:
        pl.semaphore_signal(barrier, inc=1, device_id=peer, device_id_type=MESH)

    loads = [pltpu.make_async_copy(c_hbm, c, load_sem.at[0])]
    for h in range(2):
        rows = pl.ds(16 * h, 16)
        loads.append(pltpu.make_async_copy(x_hbm.at[:, :, rows], x.at[:, :, rows], load_sem.at[1 + 2 * h]))
        loads.append(pltpu.make_async_copy(v_hbm.at[:, rows], v.at[:, rows], load_sem.at[2 + 2 * h]))
    loads.append(pltpu.make_async_copy(w_hbm, w, load_sem.at[5]))
    for load in loads:
        load.start()

    lane = lax.broadcasted_iota(jnp.int32, (16, 128), 1)
    sign = jnp.where(lane < 64, -1.0, 1.0).astype(F32)

    def pair_step(i, carry):
        ks = [i * STEP_A + u for u in range(STEP_A)]
        halves = []
        for k in ks:
            xk = jnp.concatenate([x[0, 0, k], x[1, 0, k], x[0, 1, k], x[1, 1, k]], axis=0)
            ck = jnp.concatenate([c[0, k], c[1, k]], axis=0)
            halves.append(dot(ck, xk, NT))
        lefts = []
        for h in halves:
            parts = []
            for b in range(2):
                cols = h[:, 128 * b : 128 * (b + 1)]
                q = cols[:16] + sign * pltpu.roll(cols[16:], 64, 1)
                parts += [q, pltpu.roll(q, 64, 1) * -sign]
            lefts.append(jnp.concatenate(parts, axis=0).astype(BF16))
        for k, left in zip(ks, lefts):
            vk = jnp.concatenate([v[0, k], v[1, k]], axis=0)
            pair = dot(left, vk)
            for q in range(4):
                spread.at[q][pl.ds(k, 64, stride=32), :] = pair[:, 128 * q : 128 * (q + 1)]
        return carry

    def pack_pairs(b, h):
        def step(nu, carry):
            for ri in range(2):
                start = pl.multiple_of((b * 32 + ri * 16 + nu) * 32 + 16 * h, 16)
                for q in range(4):
                    send1[b, nu, ri, pl.ds(16 * h, 16), 128 * q : 128 * (q + 1)] = spread[
                        q, pl.ds(start, 16), :
                    ].astype(BF16)
            return carry

        lax.fori_loop(0, 16, step, 0)

    def first_copy(b, h, j, src_m, dst_m, peer):
        i = (b * 2 + h) * 8 + j
        return pltpu.make_async_remote_copy(
            src_ref=send1.at[b, pl.ds(2 * dst_m, 2), :, pl.ds(16 * h, 16), :],
            dst_ref=recv1.at[b, :, :, pl.ds(pl.multiple_of(32 * src_m + 16 * h, 16), 16), :],
            send_sem=s1.at[i],
            recv_sem=r1.at[i],
            device_id=(peer, p),
            device_id_type=MESH,
        )

    firsts = []
    selfs = []
    for h in range(2):
        if h == 0:
            loads[0].wait()
        loads[1 + 2 * h].wait()
        loads[2 + 2 * h].wait()
        lax.fori_loop(h * (16 // STEP_A), (h + 1) * (16 // STEP_A), pair_step, 0)
        if h == 0:
            pl.semaphore_wait(barrier, len(peers))
        for b in range(2):
            pack_pairs(b, h)
            for j in (2, 6, 1, 5, 3, 7, 4):
                copy = first_copy(b, h, j, m, mom_to(j), mom_to(j))
                copy.start()
                firsts.append(copy)
            copy = pltpu.make_async_copy(
                send1.at[b, pl.ds(2 * m, 2), :, pl.ds(16 * h, 16), :],
                recv1.at[b, :, :, pl.ds(pl.multiple_of(32 * m + 16 * h, 16), 16), :],
                self_sem.at[b * 2 + h],
            )
            copy.start()
            selfs.append((b, copy))

    frequency = lax.broadcasted_iota(jnp.int32, (256, 256), 0)
    angle = ((frequency * grid_row[...]) & 255).astype(F32) * (2.0 * math.pi / 256)
    cosine = jnp.cos(angle)
    sine = jnp.sin(angle)
    cosine_t = cosine.T
    sine_t = sine.T
    fwd[:256, :256] = cosine.astype(BF16)
    fwd[:256, 256:] = sine.astype(BF16)
    fwd[256:, :256] = (-sine).astype(BF16)
    fwd[256:, 256:] = cosine.astype(BF16)
    scale = 1.0 / 256
    inv[:256, :256] = (cosine_t * scale).astype(BF16)
    inv[:256, 256:] = (sine_t * -scale).astype(BF16)
    inv[256:, :256] = (sine_t * scale).astype(BF16)
    inv[256:, 256:] = (cosine_t * scale).astype(BF16)

    first_row = pl.multiple_of((p // 8) * 16, 16)
    for ri in range(2):
        for b in range(2):
            piece = x[ri, b, :, pl.ds(first_row, 16), :].astype(F32)
            own_x[pl.ds((ri * 2 + b) * 512, 512), :] = piece.reshape(512, 128)
    loads[5].wait()

    def second_copy(b, nu, j, src_m, dst_m, peer):
        i = (b * 2 + nu) * 8 + j
        return pltpu.make_async_remote_copy(
            src_ref=send2.at[b, nu, :, pl.ds(pl.multiple_of(32 * dst_m, 32), 32), :],
            dst_ref=recv2.at[b, 2 * src_m + nu],
            send_sem=s2.at[i],
            recv_sem=r2.at[i],
            device_id=(peer, p),
            device_id_type=MESH,
        )

    seconds = []
    for b in range(2):
        for owner, copy in selfs:
            if owner == b:
                copy.wait()
        for h in range(2):
            for j in range(1, 8):
                first_copy(b, h, j, mom_from(j), m, mom_to(j)).wait_recv()
        for nu in range(2):

            def transform(i, carry, b=b, nu=nu):
                cols = pl.ds(pl.multiple_of(i * 256, 256), 256)
                spec = dot(fwd[...], recv1[b, nu, :, :, cols].reshape(512, 256))
                real, imag = spec[:256], spec[256:]
                wr = w[nu, 0, :, cols].astype(F32)
                wi = w[nu, 1, :, cols].astype(F32)
                prod = jnp.concatenate([wr * real - wi * imag, wr * imag + wi * real], axis=0)
                back = dot(inv[...], prod.astype(BF16))
                send2[b, nu, :, :, cols] = back.astype(BF16).reshape(2, 256, 256)
                return carry

            lax.fori_loop(0, 2, transform, 0)
            for j in (2, 6, 1, 5, 3, 7, 4):
                copy = second_copy(b, nu, j, m, mom_to(j), mom_to(j))
                copy.start()
                seconds.append(copy)
            copy = pltpu.make_async_copy(
                send2.at[b, nu, :, pl.ds(pl.multiple_of(32 * m, 32), 32), :],
                recv2.at[b, 2 * m + nu],
                self_sem.at[4 + b * 2 + nu],
            )
            copy.start()
            selfs.append((2 + b, copy))

    def band_step(b):
        def step(i, carry):
            ks = [i * STEP_D + u for u in range(STEP_D)]
            mixed = []
            for k in ks:
                left = jnp.concatenate(
                    [spread.at[q][pl.ds(b * 1024 + k, 32, stride=32), :] for q in range(4)], axis=1
                ).astype(BF16)
                vk = jnp.concatenate([v[0, k], v[1, k]], axis=0)
                mixed.append(dot(left, vk, NT))
            lefts = []
            for o in mixed:
                q = o[:16] + sign * pltpu.roll(o[16:], 64, 1)
                lefts.append(jnp.concatenate([q, pltpu.roll(q, 64, 1) * -sign], axis=0).astype(BF16))
            for k, left in zip(ks, lefts):
                ck = jnp.concatenate([c[0, k], c[1, k]], axis=0)
                band.at[b][pl.ds(k, 128, stride=32), :] = dot(left, ck, TN)
            return carry

        return step

    def piece_rows(ri, y, z, core):
        return pl.ds(pl.multiple_of(((ri * 4 + y) * 4 + z) * 128 + core * 64, 64), 64)

    def remote(src, dst, send, recv, peer):
        return pltpu.make_async_remote_copy(
            src_ref=src, dst_ref=dst, send_sem=send, recv_sem=recv, device_id=peer, device_id_type=MESH
        )

    swaps = []
    later = []
    for b in range(2):
        for owner, copy in selfs:
            if owner == 2 + b:
                copy.wait()
        for nu in range(2):
            for j in range(1, 8):
                second_copy(b, nu, j, mom_from(j), m, mom_to(j)).wait_recv()

        def unpack(nu, carry, b=b):
            for ri in range(2):
                start = pl.multiple_of(b * 1024 + (ri * 16 + nu) * 32, 32)
                for q in range(4):
                    spread[q, pl.ds(start, 32), :] = recv2[
                        b, nu, ri, :, 128 * q : 128 * (q + 1)
                    ].astype(F32)
            return carry

        lax.fori_loop(0, 16, unpack, 0)
        lax.fori_loop(0, 32 // STEP_D, band_step(b), 0)

        for ri in range(2):
            for y in range(4):
                for z in range(4):
                    send_c[b, ri, y, z] = band[b, piece_rows(ri, y, z, 1 - pc), :].astype(BF16)
        core_copy = remote(send_c.at[b], recv_c.at[b], sc.at[b], rc.at[b], core_peer)
        core_copy.start()
        core_copy.wait_recv()
        later.append(core_copy)
        y_copies = []
        for d in (2, 1, 3, 0):
            yy = (py + d) % 4
            for ri in range(2):
                for z in range(4):
                    part = band[b, piece_rows(ri, yy, z, pc), :] + recv_c[b, ri, yy, z].astype(F32)
                    if d == 0:
                        own_y[ri, z] = part
                    else:
                        send_y[b, d - 1, ri, z] = part.astype(BF16)
            if d:
                copy = remote(
                    send_y.at[b, d - 1], recv_y.at[b, d - 1], sy.at[b * 3 + d - 1], ry.at[b * 3 + d - 1], y_to(d)
                )
                copy.start()
                y_copies.append(copy)
        for copy in y_copies:
            copy.wait_recv()
        later += y_copies
        z_copies = []
        for d in (2, 1, 3, 0):
            zz = (ph + d) % 4
            for ri in range(2):
                part = own_y[ri, zz]
                for i in range(3):
                    part += recv_y[b, i, ri, zz].astype(F32)
                if d == 0:
                    own_z[ri] = part
                else:
                    send_z[b, d - 1, ri] = part.astype(BF16)
            if d:
                copy = remote(
                    send_z.at[b, d - 1], recv_z.at[b, d - 1], sz.at[b * 3 + d - 1], rz.at[b * 3 + d - 1], z_to(d)
                )
                copy.start()
                z_copies.append(copy)
        for copy in z_copies:
            copy.wait_recv()
        later += z_copies
        for ri in range(2):
            part = own_z[ri]
            for i in range(3):
                part += recv_z[b, i, ri].astype(F32)
            total[b, ri] = part
            send_p[b, ri] = part.astype(BF16)
        swap = remote(send_p.at[b], recv_p.at[b], sp.at[b], rp.at[b], swap_peer)
        swap.start()
        swaps.append(swap)

    slot = lax.broadcasted_iota(jnp.int32, (32, 32), 0)
    pick = jnp.where(slot == (opp_row[...] & 31), 1.0, 0.0).astype(BF16)
    across = lax.broadcasted_iota(jnp.int32, (32, 32), 1)
    for swap in swaps:
        swap.wait_recv()
    for row in range(2):
        energy = jnp.sum(jnp.where(slot == across, val_e[row : row + 1, :], 0.0), axis=1, keepdims=True)
        gap = cond_e[...] - energy
        rows = pl.ds(row * 32, 32)
        for b in range(2):
            for ri in range(2):
                own = own_x[pl.ds((ri * 2 + b) * 512 + 2 * (p % 8) + row, 32, stride=16), :]
                mirrored = dot(pick, recv_p[1 - b, ri, rows, :], TN)
                here = total[b, ri, rows, :]
                turned = mirrored if ri == 0 else -mirrored
                result = gap * own - here - turned
                if b == 1:
                    result = -gap * own + here + turned
                out[pl.ds((ri * 2 + b) * 64 + row, 32, stride=2), :] = result

    for copy in firsts + seconds + later + swaps:
        copy.wait_send()


def on_device(
    amplitudes, val_orbitals, cond_orbitals, screened, val_energy, cond_energy, grid_of_slot, opposite_slot
):
    weights = jnp.transpose(screened, (2, 0, 1, 3))
    hbm = pl.BlockSpec(memory_space=pl.ANY)
    vmem = pl.BlockSpec(memory_space=pltpu.VMEM)
    dma = pltpu.SemaphoreType.DMA
    out = pl.pallas_call(
        kernel,
        out_shape=jax.ShapeDtypeStruct((256, 128), F32),
        in_specs=[hbm] * 4 + [vmem] * 4,
        out_specs=vmem,
        scratch_shapes=[
            pltpu.VMEM((2, 2, 32, 64, 128), BF16),
            pltpu.VMEM((2, 32, 64, 512), BF16),
            pltpu.VMEM((2, 32, 16, 128), BF16),
            pltpu.VMEM((2, 2, 256, 512), BF16),
            pltpu.VMEM((512, 512), BF16),
            pltpu.VMEM((512, 512), BF16),
            pltpu.VMEM((4, 2048, 128), F32),
            pltpu.VMEM((2, 16, 2, 32, 512), BF16),
            pltpu.VMEM((2, 2, 2, 256, 512), BF16),
            pltpu.VMEM((2, 2, 2, 256, 512), BF16),
            pltpu.VMEM((2, 16, 2, 32, 512), BF16),
            pltpu.VMEM((2, 4096, 128), F32),
            pltpu.VMEM((2048, 128), F32),
            pltpu.VMEM((2, 2, 4, 4, 64, 128), BF16),
            pltpu.VMEM((2, 2, 4, 4, 64, 128), BF16),
            pltpu.VMEM((2, 4, 64, 128), F32),
            pltpu.VMEM((2, 3, 2, 4, 64, 128), BF16),
            pltpu.VMEM((2, 3, 2, 4, 64, 128), BF16),
            pltpu.VMEM((2, 64, 128), F32),
            pltpu.VMEM((2, 3, 2, 64, 128), BF16),
            pltpu.VMEM((2, 3, 2, 64, 128), BF16),
            pltpu.VMEM((2, 2, 64, 128), F32),
            pltpu.VMEM((2, 2, 64, 128), BF16),
            pltpu.VMEM((2, 2, 64, 128), BF16),
            dma((6,)), dma((8,)), dma((32,)), dma((32,)), dma((32,)), dma((32,)),
            dma((2,)), dma((2,)), dma((6,)), dma((6,)), dma((6,)), dma((6,)), dma((2,)), dma((2,)),
        ],
        compiler_params=pltpu.CompilerParams(
            collective_id=0, has_side_effects=True, vmem_limit_bytes=56 * 2**20
        ),
        cost_estimate=pl.CostEstimate(flops=2800000000, bytes_accessed=8000000, transcendentals=131072),
    )(
        amplitudes.reshape(2, 2, 32, 64, 128),
        val_orbitals,
        cond_orbitals,
        weights,
        val_energy.T,
        cond_energy,
        grid_of_slot.reshape(1, 256),
        opposite_slot.reshape(1, 32),
    )
    return out.reshape(2, 2, 1, 32, 2, 128)


def solution(mesh):
    in_specs = (
        P(None, None, None, "mom", None, None),
        P(None, "mom", None, None),
        P(None, "mom", "pts", None),
        P(None, None, ("pts", "mom"), None),
        P("mom", "pts"),
        P("mom", None),
        P(),
        P("mom"),
    )
    out_specs = P(None, None, None, "mom", "pts", None)
    return jax.shard_map(
        on_device, mesh=mesh, in_specs=in_specs, out_specs=out_specs, check_vma=False
    )
```

time: 288 us -> 103 us (0.36); the launches traced: 284 us -> 103 us
  waiting for transfers between devices: 120 us -> 0 us
  Pallas kernels: 0 us -> 98.5 us
  local copies, waits for them, and re-layouts: 63.2 us -> 3.96 us
  matrix products: 29.7 us -> 0 us
  blocking collectives: 29.4 us -> 0 us
  other arithmetic: 21.4 us -> 0 us
  between operations: 13.7 us -> 0.01 us
  starting transfers between devices: 7.02 us -> 0 us
    pallas_call x0 -> x1, Pallas kernels: none -> 98.5 us  [on_device(): pl.pallas_call(kernel, out_shape=jax.ShapeDtypeStruct((256, 128), F32), i...]
    reduce_scatter x1 -> x0, waiting for transfers between devices: 98 us -> none  [on_device(): lax.psum_scatter(band_terms, 'pts', scatter_dimension=4, tiled=True)]
    dot_general x24 -> x0, matrix products: 29.7 us -> none  [the longest x4 5 us: complex_mix(): jnp.einsum(formula, left[1], right[0], preferred_element_type=jnp.float32)]
    all_to_all x1 -> x0, blocking collectives: 29.4 us -> none  [on_device(): lax.all_to_all(jnp.stack([back_real, back_imag]).astype(jnp.bfloat16), 'm...]
    all_to_all x1 -> x0, waiting for transfers between devices: 20.1 us -> none  [on_device(): lax.all_to_all(flattened, 'mom', split_axis=4, concat_axis=3, tiled=True)]
    another operation x6 -> x0, local copies, waits for them, and re-layouts: 19.1 us -> none  [the longest x3 14.2 us: complex_mix(): jnp.stack([real_real - left_sign * right_sign * imag_imag, right_sign * r...]
    unnamed x1 -> x0, other arithmetic: 16.3 us -> none
    unnamed x27 -> x2, local copies, waits for them, and re-layouts: 19.8 us -> 3.96 us
  transfers between devices with their start and end apart: 3 -> 0, of which waited for: 3 -> 0; matrix products, arithmetic and copies ran while one was open for 3% -> 0% of each run, Pallas kernels for 0% -> 0%
where the time goes in v1:
time: 103 us
  Pallas kernels  98.5 us (96%)
  local copies, waits for them, and re-layouts  3.96 us (4%)
    pallas_call x1, Pallas kernels, on_device(): pl.pallas_call(kernel, out_shape=jax.ShapeDtypeStruct((256, 128), F32), i...  98.5 us
    unnamed x2, local copies, waits for them, and re-layouts  3.96 us

profile of v1, /device:TPU:1, one launch (start us, length us, event | category | flops | bytes accessed | tf_op | source)
XLA Modules:
  0.0 102.5 jit_solution(15724305501918657772)
XLA Ops:
  0.0 2.4 %copy.12 = bf16[2,256,2,512]{3,1,0,2:T(8,128)(2,1)} copy(bf16[2,256,2,512]{3,2,1,0:T(2,128)(2,1)} %param.11) | data formatting | bytes 2097152 | tf_op args[3]
  2.4 98.5 %shard_map.82 = f32[256,128]{1,0:T(8,128)} custom-call(bf16[2,2,32,64,128]{4,3,2,1,0:T(8,128)(2,1)} %bitcast.12, bf16[2,32,64,512]{3,2,1,0:T(8,128)(2,1)} %v_hbm.1, bf16[2,32,16,128]{3,2,1,0:T(8,128)(2,1)} %c_hbm.1, bf16[2,2,256,512]{3,2,1,0:T(8,128)(2,1)} %bitcast.10, f32[2,32]{1,0:T(2,128)} %bitcast.13, f32[32,128]{1,0:T(8,128)} %cond_e.1, ...), custom_call_target="tpu_custom_call" | custom-call | flops 2800000000 | bytes 8000000 | tf_op jit(solution)/shard_map/pallas_call | solution.py:345
  100.9 1.6 %copy.14 = f32[2,2,1,32,2,128]{5,4,3,2,1,0:T(2,128)} copy(f32[2,2,1,32,2,128]{5,4,3,2,1,0:T(2,128)} %bitcast.11) | data formatting | bytes 262144

commit v2 on v0

v2 whole, which is shorter than its diff:
```python
import math

import jax
import jax.numpy as jnp
from jax import lax
from jax.experimental import pallas as pl
from jax.experimental.pallas import tpu as pltpu
from jax.sharding import PartitionSpec as P

MESH = pl.DeviceIdType.MESH
F32 = jnp.float32
BF16 = jnp.bfloat16
NT = (((1,), (1,)), ((), ()))
TN = (((0,), (0,)), ((), ()))
ORDER = (2, 6, 1, 5, 3, 7, 4)


def dot(a, b, dims=(((1,), (0,)), ((), ()))):
    return lax.dot_general(a, b, dims, preferred_element_type=F32)


def aligned(value, by):
    return pl.multiple_of(value, by)


def kernel(
    x_hbm, v_hbm, c_hbm, w_hbm, val_e, cond_e, grid_row, opp_row,
    out,
    x, v, c, c_both, w, w32, fwd, inv, spread, send1, recv1, send2, recv2, band, own_x,
    send_y, recv_y, own_z, send_z, recv_z, total, peer_total, send_p, recv_p, full, mirror,
    load_sem, self_sem, s0, r0, s1, r1, s2, r2, sy, ry, sz, rz, sp, rp, st, rt,
):
    m = lax.axis_index("mom")
    p = lax.axis_index("pts")
    mx, mz = m % 4, m // 4
    py, ph, pc = p // 8, (p // 2) % 4, p % 2
    p_other = p + 1 - 2 * pc

    def mom_to(j):
        return ((mz + j // 4) % 2) * 4 + (mx + j % 4) % 4

    def mom_from(j):
        return ((mz + j // 4) % 2) * 4 + (mx + 4 - j % 4) % 4

    def pts_of(e):
        return p_other if e else p

    def core_of(e):
        return 1 - pc if e else pc

    def y_to(d):
        return (m, ((py + d) % 4) * 8 + p % 8)

    def z_to(d):
        return (m, py * 8 + ((ph + d) % 4) * 2 + pc)

    def remote(src, dst, send, recv, peer):
        return pltpu.make_async_remote_copy(
            src_ref=src, dst_ref=dst, send_sem=send, recv_sem=recv, device_id=peer, device_id_type=MESH
        )

    def load_x(ch):
        rows = pl.ds(8 * ch, 8)
        return pltpu.make_async_copy(x_hbm.at[:, :, rows], x.at[:, :, rows], load_sem.at[ch])

    def load_v(ch):
        rows = pl.ds(8 * ch, 8)
        return pltpu.make_async_copy(v_hbm.at[:, rows], v.at[:, rows], load_sem.at[4 + ch])

    load_c = pltpu.make_async_copy(c_hbm, c, load_sem.at[8])
    load_w = pltpu.make_async_copy(w_hbm, w, load_sem.at[9])
    load_c.start()
    for ch in range(4):
        load_x(ch).start()
        load_v(ch).start()
    load_w.start()

    barrier = pltpu.get_barrier_semaphore()
    peers = [(mom_to(j), pts_of(e)) for j in range(8) for e in range(2) if j + e]
    peers += [y_to(d) for d in range(1, 4)] + [z_to(d) for d in range(1, 4)]
    for peer in peers:
        pl.semaphore_signal(barrier, inc=1, device_id=peer, device_id_type=MESH)

    lane = lax.broadcasted_iota(jnp.int32, (32, 128), 1)
    sign = jnp.where(lane < 64, -1.0, 1.0).astype(F32)

    def first_copy(b, ch, j, src_m, dst_m, peer):
        i = (b * 4 + ch) * 8 + j
        return remote(
            send1.at[b, ch, pl.ds(2 * dst_m, 2)],
            recv1.at[b, :, pl.ds(aligned((src_m * 4 + ch) * 16, 16), 16), :],
            s1.at[i],
            r1.at[i],
            (peer, p),
        )

    def first_self(b, ch):
        return pltpu.make_async_copy(
            send1.at[b, ch, pl.ds(2 * m, 2)],
            recv1.at[b, :, pl.ds(aligned((m * 4 + ch) * 16, 16), 16), :],
            self_sem.at[b * 4 + ch],
        )

    def send_first(b, ch):
        for j in ORDER:
            first_copy(b, ch, j, m, mom_to(j), mom_to(j)).start()
        first_self(b, ch).start()

    def pair_chunk(ch, carry):
        load_x(ch).wait()
        load_v(ch).wait()
        for group in range(2):
            ks = [group * 4 + u for u in range(4)]
            halves = []
            for k8 in ks:
                k = ch * 8 + k8
                xk = jnp.concatenate([x[0, 0, k], x[1, 0, k], x[0, 1, k], x[1, 1, k]], axis=0)
                ck = jnp.concatenate([c[0, k], c[1, k]], axis=0)
                halves.append(dot(ck, xk, NT))
            lefts = []
            for h in halves:
                parts = []
                for b in range(2):
                    cols = h[:, 128 * b : 128 * (b + 1)]
                    q = cols[:16] + sign[:16] * pltpu.roll(cols[16:], 64, 1)
                    parts += [q, pltpu.roll(q, 64, 1) * -sign[:16]]
                lefts.append(jnp.concatenate(parts, axis=0).astype(BF16))
            for k8, left in zip(ks, lefts):
                k = ch * 8 + k8
                pair = dot(left, jnp.concatenate([v[0, k], v[1, k]], axis=0))
                for b in range(2):
                    for ri in range(2):
                        top = (b * 2 + ri) * 16
                        for q in range(4):
                            spread.at[q][pl.ds(b * 256 + ri * 8 + k8, 16, stride=16), :] = pair[
                                top : top + 16, 128 * q : 128 * (q + 1)
                            ]
        for b in range(2):
            for q in range(4):
                send1[b, ch, :, :, 128 * q : 128 * (q + 1)] = (
                    spread[q, 256 * b : 256 * (b + 1), :].astype(BF16).reshape(16, 16, 128)
                )
        send_first(0, ch)
        return carry

    load_c.wait()
    pl.semaphore_wait(barrier, len(peers))
    half = pl.ds(16 * (1 - pc), 16)
    points = pl.ds(aligned(16 * pc, 16), 16)
    points_other = pl.ds(aligned(16 * (1 - pc), 16), 16)
    share_c = remote(c.at[:, half], c_both.at[:, :, points], s0, r0, (m, p_other))
    share_c.start()
    lax.fori_loop(0, 4, pair_chunk, 0)
    c_both[:, :, points] = c[:, pl.ds(16 * pc, 16)]

    def make_tables():
        frequency = lax.broadcasted_iota(jnp.int32, (256, 256), 0)
        angle = ((frequency * grid_row[...]) & 255).astype(F32) * (2.0 * math.pi / 256)
        slot = lax.broadcasted_iota(jnp.int32, (256, 512), 0)
        column = lax.broadcasted_iota(jnp.int32, (256, 512), 1)
        place = jnp.where(slot == (column >> 4) * 8 + (column & 7), 1.0, 0.0).astype(BF16)
        cosine = dot(jnp.cos(angle).astype(BF16), place)
        sine = dot(jnp.sin(angle).astype(BF16), place)
        real = (column & 8) == 0
        top = jnp.where(real, cosine, sine)
        bottom = jnp.where(real, -sine, cosine)
        fwd[:256, :] = top.astype(BF16)
        fwd[256:, :] = bottom.astype(BF16)
        inv[:, :256] = (top.T * (1.0 / 256)).astype(BF16)
        inv[:, 256:] = (bottom.T * (1.0 / 256)).astype(BF16)

    make_tables()
    first_row = aligned((p // 8) * 16, 16)
    for ri in range(2):
        for b in range(2):
            piece = x[ri, b, :, pl.ds(first_row, 16), :].astype(F32)
            own_x[pl.ds((ri * 2 + b) * 512, 512), :] = piece.reshape(512, 128)
    load_w.wait()
    w32[...] = w[...].astype(F32)

    def second_copy(b, kk, j, e, src_m, src_c, dst_m, dst_c, peer):
        i = ((b * 2 + kk) * 8 + j) * 2 + e
        return remote(
            send2.at[b, :, pl.ds(aligned(((dst_m * 2 + dst_c) * 2 + kk) * 16, 16), 16), :],
            recv2.at[b, kk, pl.ds(16 * src_c + 2 * src_m, 2)],
            s2.at[i],
            r2.at[i],
            peer,
        )

    def second_to(b, kk, j, e):
        return second_copy(b, kk, j, e, m, pc, mom_to(j), core_of(e), (mom_to(j), pts_of(e)))

    def second_from(b, kk, j, e):
        return second_copy(b, kk, j, e, mom_from(j), core_of(e), m, pc, (mom_to(j), pts_of(e)))

    def second_self(b, kk):
        return pltpu.make_async_copy(
            send2.at[b, :, pl.ds(aligned(((m * 2 + pc) * 2 + kk) * 16, 16), 16), :],
            recv2.at[b, kk, pl.ds(16 * pc + 2 * m, 2)],
            self_sem.at[8 + b * 2 + kk],
        )

    def send_second(b, kk):
        for j in ORDER + (0,):
            for e in range(2):
                if j + e:
                    second_to(b, kk, j, e).start()
        second_self(b, kk).start()

    def second_sent(b, kk):
        for j in ORDER + (0,):
            for e in range(2):
                if j + e:
                    second_to(b, kk, j, e).wait_send()

    def first_sent(b, ch):
        for j in ORDER:
            first_copy(b, ch, j, m, mom_to(j), mom_to(j)).wait_send()

    def first_arrived(b):
        def step(ch, carry):
            for j in range(1, 8):
                first_copy(b, ch, j, mom_from(j), m, mom_to(j)).wait_recv()
            first_self(b, ch).wait()
            return carry

        lax.fori_loop(0, 4, step, 0)

    def transform_block(b):
        def transform(i, carry):
            nu, half = i // 2, i % 2
            cols = pl.ds(aligned(half * 256, 256), 256)
            spec = dot(fwd[...], recv1[b, nu, :, cols])
            real, imag = spec[:256], spec[256:]

            def weight(ri):
                return jnp.concatenate(
                    [w32[pl.ds(ri * 2048 + (2 * half + t) * 2 + nu, 256, stride=8), :] for t in range(2)], axis=1
                )

            wr, wi = weight(0), weight(1)
            prod = jnp.concatenate([wr * real - wi * imag, wr * imag + wi * real], axis=0)
            send2[b, nu, :, cols] = dot(inv[...], prod.astype(BF16)).astype(BF16)
            return carry

        lax.fori_loop(0, 4, transform, 0)

    def resend(ch, carry):
        first_sent(0, ch)
        send_first(1, ch)
        return carry

    lax.fori_loop(0, 4, resend, 0)
    first_arrived(0)
    transform_block(0)
    first_sent(1, 0)
    first_sent(1, 1)
    send_second(0, 0)
    first_sent(1, 2)
    first_sent(1, 3)
    send_second(0, 1)
    first_arrived(1)
    transform_block(1)
    second_sent(0, 0)
    send_second(1, 0)
    share_c.wait_send()
    remote(c.at[:, half], c_both.at[:, :, points_other], s0, r0, (m, p_other)).wait_recv()

    def second_arrived(b, kk):
        for j in range(8):
            for e in range(2):
                if j + e:
                    second_from(b, kk, j, e).wait_recv()
        second_self(b, kk).wait()

    def band_unit(b, kk):
        for q in range(4):
            spread[q] = recv2[b, kk, :, :, 128 * q : 128 * (q + 1)].astype(F32).reshape(512, 128)
        mixed = []
        for k8 in range(8):
            rows = [
                jnp.concatenate(
                    [spread.at[q][pl.ds(ri * 8 + k8, 32, stride=16), :] for q in range(4)], axis=1
                )
                for ri in range(2)
            ]
            k = 16 * pc + 8 * kk + k8
            vk = jnp.concatenate([v[0, k], v[1, k]], axis=0)
            mixed.append(dot(jnp.concatenate(rows, axis=0).astype(BF16), vk, NT))
        lefts = []
        for o in mixed:
            q = o[:32] + sign * pltpu.roll(o[32:], 64, 1)
            lefts.append(jnp.concatenate([q, pltpu.roll(q, 64, 1) * -sign], axis=0).astype(BF16))
        for k8, left in enumerate(lefts):
            ck = jnp.concatenate([c_both[0, 8 * kk + k8], c_both[1, 8 * kk + k8]], axis=0)
            band.at[b * 2 + kk][pl.ds(k8, 128, stride=8), :] = dot(left, ck, TN)

    def y_copy(u, d):
        i = u * 3 + d - 1
        return remote(send_y.at[u, d - 1], recv_y.at[u, d - 1], sy.at[i], ry.at[i], y_to(d))

    def z_copy(u, d):
        i = u * 3 + d - 1
        return remote(send_z.at[u, d - 1], recv_z.at[u, d - 1], sz.at[i], rz.at[i], z_to(d))

    def y_start(u):
        for d in (2, 1, 3):
            for ri in range(2):
                row = aligned(ri * 512 + ((py + d) % 4) * 128, 128)
                send_y[u, d - 1, ri] = band[u, pl.ds(row, 128), :].astype(BF16)
            y_copy(u, d).start()

    def z_start(u):
        for d in range(1, 4):
            y_copy(u, d).wait_recv()
        for d in (2, 1, 3, 0):
            zz = aligned(((ph + d) % 4) * 32, 32)
            for ri in range(2):
                part = band[u, pl.ds(aligned(ri * 512 + py * 128 + zz, 32), 32), :]
                for i in range(3):
                    part += recv_y[u, i, ri, pl.ds(zz, 32), :].astype(F32)
                if d == 0:
                    own_z[u, ri] = part
                else:
                    send_z[u, d - 1, ri] = part.astype(BF16)
            if d:
                z_copy(u, d).start()

    def finish(u):
        for d in range(1, 4):
            z_copy(u, d).wait_recv()
        b, kk = u // 2, u % 2
        for ri in range(2):
            part = own_z[u, ri]
            for i in range(3):
                part += recv_z[u, i, ri].astype(F32)
            total[u, ri] = part.reshape(2, 16, 128)
            for e in range(2):
                send_p[b, e, kk, ri] = total[u, ri, core_of(e)].astype(BF16)

    def swap_from(b, e):
        return remote(
            send_p.at[b, e],
            recv_p.at[b, core_of(e)],
            sp.at[b * 2 + e],
            rp.at[b * 2 + e],
            ((m + 4) % 8, pts_of(e)),
        )

    def core_copy(b):
        return remote(
            total.at[pl.ds(2 * b, 2), :, 1 - pc], peer_total.at[pl.ds(2 * b, 2)], st.at[b], rt.at[b], (m, p_other)
        )

    def swap_start(b):
        for e in range(2):
            remote(
                send_p.at[b, e], recv_p.at[b, pc], sp.at[b * 2 + e], rp.at[b * 2 + e], ((m + 4) % 8, pts_of(e))
            ).start()
        core_copy(b).start()

    second_arrived(0, 0)
    band_unit(0, 0)
    y_start(0)
    second_sent(0, 1)
    send_second(1, 1)
    second_arrived(0, 1)
    band_unit(0, 1)
    y_start(1)
    z_start(0)
    second_arrived(1, 0)
    band_unit(1, 0)
    y_start(2)
    z_start(1)
    finish(0)
    second_arrived(1, 1)
    band_unit(1, 1)
    y_start(3)
    z_start(2)
    finish(1)
    swap_start(0)
    z_start(3)
    finish(2)
    finish(3)
    swap_start(1)

    slot = lax.broadcasted_iota(jnp.int32, (32, 32), 0)
    pick = jnp.where(slot == (opp_row[...] & 31), 1.0, 0.0).astype(BF16)
    across = lax.broadcasted_iota(jnp.int32, (32, 32), 1)
    gaps = []
    for row in range(2):
        energy = jnp.sum(jnp.where(slot == across, val_e[row : row + 1, :], 0.0), axis=1, keepdims=True)
        gaps.append(cond_e[...] - energy)
    for b in range(2):
        core_copy(b).wait_recv()
        for e in range(2):
            swap_from(b, e).wait_recv()
        for ri in range(2):
            for kk in range(2):
                for row in range(2):
                    part = slice(8 * row, 8 * row + 8)
                    u = b * 2 + kk
                    full[b, ri, row, pl.ds(aligned(16 * pc + 8 * kk, 8), 8), :] = total[u, ri, pc, part]
                    full[b, ri, row, pl.ds(aligned(16 * (1 - pc) + 8 * kk, 8), 8), :] = peer_total[u, ri, part]
                    for core in range(2):
                        mirror[b, ri, row, 16 * core + 8 * kk : 16 * core + 8 * kk + 8, :] = recv_p[
                            b, core, kk, ri
                        ].astype(F32)[part]
    for row in range(2):
        for b in range(2):
            for ri in range(2):
                own = own_x[pl.ds((ri * 2 + b) * 512 + 2 * (p % 8) + row, 32, stride=16), :]
                mirrored = dot(pick, mirror[1 - b, ri, row].astype(BF16), TN)
                here = full[b, ri, row]
                turned = mirrored if ri == 0 else -mirrored
                result = gaps[row] * own - here - turned
                if b == 1:
                    result = -gaps[row] * own + here + turned
                out[pl.ds((ri * 2 + b) * 64 + row, 32, stride=2), :] = result

    second_sent(1, 0)
    second_sent(1, 1)
    for u in range(4):
        for d in range(1, 4):
            y_copy(u, d).wait_send()
            z_copy(u, d).wait_send()
    for b in range(2):
        core_copy(b).wait_send()
        for e in range(2):
            swap_from(b, e).wait_send()


def on_device(
    amplitudes, val_orbitals, cond_orbitals, screened, val_energy, cond_energy, grid_of_slot, opposite_slot
):
    weights = screened.reshape(2, 256, 2, 4, 128).transpose(0, 1, 3, 2, 4).reshape(4096, 128)
    hbm = pl.BlockSpec(memory_space=pl.ANY)
    vmem = pl.BlockSpec(memory_space=pltpu.VMEM)
    dma = pltpu.SemaphoreType.DMA
    out = pl.pallas_call(
        kernel,
        out_shape=jax.ShapeDtypeStruct((256, 128), F32),
        in_specs=[hbm] * 4 + [vmem] * 4,
        out_specs=vmem,
        scratch_shapes=[
            pltpu.VMEM((2, 2, 32, 64, 128), BF16),
            pltpu.VMEM((2, 32, 64, 512), BF16),
            pltpu.VMEM((2, 32, 16, 128), BF16),
            pltpu.VMEM((2, 16, 32, 128), BF16),
            pltpu.VMEM((4096, 128), BF16),
            pltpu.VMEM((4096, 128), F32),
            pltpu.VMEM((512, 512), BF16),
            pltpu.VMEM((512, 512), BF16),
            pltpu.VMEM((4, 512, 128), F32),
            pltpu.VMEM((2, 4, 16, 16, 512), BF16),
            pltpu.VMEM((2, 2, 512, 512), BF16),
            pltpu.VMEM((2, 2, 512, 512), BF16),
            pltpu.VMEM((2, 2, 32, 16, 512), BF16),
            pltpu.VMEM((4, 1024, 128), F32),
            pltpu.VMEM((2048, 128), F32),
            pltpu.VMEM((4, 3, 2, 128, 128), BF16),
            pltpu.VMEM((4, 3, 2, 128, 128), BF16),
            pltpu.VMEM((4, 2, 32, 128), F32),
            pltpu.VMEM((4, 3, 2, 32, 128), BF16),
            pltpu.VMEM((4, 3, 2, 32, 128), BF16),
            pltpu.VMEM((4, 2, 2, 16, 128), F32),
            pltpu.VMEM((4, 2, 16, 128), F32),
            pltpu.VMEM((2, 2, 2, 2, 16, 128), BF16),
            pltpu.VMEM((2, 2, 2, 2, 16, 128), BF16),
            pltpu.VMEM((2, 2, 2, 32, 128), F32),
            pltpu.VMEM((2, 2, 2, 32, 128), F32),
            dma((10,)), dma((12,)), dma, dma, dma((64,)), dma((64,)), dma((64,)), dma((64,)),
            dma((12,)), dma((12,)), dma((12,)), dma((12,)), dma((4,)), dma((4,)), dma((2,)), dma((2,)),
        ],
        compiler_params=pltpu.CompilerParams(
            collective_id=0, has_side_effects=True, vmem_limit_bytes=56 * 2**20
        ),
        cost_estimate=pl.CostEstimate(flops=2800000000, bytes_accessed=8000000, transcendentals=131072),
    )(
        amplitudes.reshape(2, 2, 32, 64, 128),
        val_orbitals,
        cond_orbitals,
        weights,
        val_energy.T,
        cond_energy,
        grid_of_slot.reshape(1, 256),
        opposite_slot.reshape(1, 32),
    )
    return out.reshape(2, 2, 1, 32, 2, 128)


def solution(mesh):
    in_specs = (
        P(None, None, None, "mom", None, None),
        P(None, "mom", None, None),
        P(None, "mom", "pts", None),
        P(None, None, ("pts", "mom"), None),
        P("mom", "pts"),
        P("mom", None),
        P(),
        P("mom"),
    )
    out_specs = P(None, None, None, "mom", "pts", None)
    return jax.shard_map(
        on_device, mesh=mesh, in_specs=in_specs, out_specs=out_specs, check_vma=False
    )
```

time: 288 us -> 80.3 us (0.28); the launches traced: 284 us -> 80.1 us
  waiting for transfers between devices: 120 us -> 0 us
  Pallas kernels: 0 us -> 78.6 us
  local copies, waits for them, and re-layouts: 63.2 us -> 1.57 us
  matrix products: 29.7 us -> 0 us
  blocking collectives: 29.4 us -> 0 us
  other arithmetic: 21.4 us -> 0 us
  between operations: 13.7 us -> 0.01 us
  starting transfers between devices: 7.02 us -> 0 us
    reduce_scatter x1 -> x0, waiting for transfers between devices: 98 us -> none  [on_device(): lax.psum_scatter(band_terms, 'pts', scatter_dimension=4, tiled=True)]
    pallas_call x0 -> x1, Pallas kernels: none -> 78.6 us  [on_device(): pl.pallas_call(kernel, out_shape=jax.ShapeDtypeStruct((256, 128), F32), i...]
    dot_general x24 -> x0, matrix products: 29.7 us -> none  [the longest x4 5 us: complex_mix(): jnp.einsum(formula, left[1], right[0], preferred_element_type=jnp.float32)]
    all_to_all x1 -> x0, blocking collectives: 29.4 us -> none  [on_device(): lax.all_to_all(jnp.stack([back_real, back_imag]).astype(jnp.bfloat16), 'm...]
    all_to_all x1 -> x0, waiting for transfers between devices: 20.1 us -> none  [on_device(): lax.all_to_all(flattened, 'mom', split_axis=4, concat_axis=3, tiled=True)]
    another operation x6 -> x0, local copies, waits for them, and re-layouts: 19.1 us -> none  [the longest x3 14.2 us: complex_mix(): jnp.stack([real_real - left_sign * right_sign * imag_imag, right_sign * r...]
    unnamed x27 -> x1, local copies, waits for them, and re-layouts: 19.8 us -> 1.57 us
    unnamed x1 -> x0, other arithmetic: 16.3 us -> none
  transfers between devices with their start and end apart: 3 -> 0, of which waited for: 3 -> 0; matrix products, arithmetic and copies ran while one was open for 3% -> 0% of each run, Pallas kernels for 0% -> 0%
where the time goes in v2:
time: 80.3 us; the launch traced here: 80.1 us
  Pallas kernels  78.6 us (98%)
  local copies, waits for them, and re-layouts  1.57 us (2%)
    pallas_call x1, Pallas kernels, on_device(): pl.pallas_call(kernel, out_shape=jax.ShapeDtypeStruct((256, 128), F32), i...  78.6 us

profile of v2, /device:TPU:1, one launch (start us, length us, event | category | flops | bytes accessed | tf_op | source)
XLA Modules:
  0.0 80.1 jit_solution(15612583921547139567)
XLA Ops:
  0.0 78.6 %shard_map.82 = f32[256,128]{1,0:T(8,128)} custom-call(bf16[2,2,32,64,128]{4,3,2,1,0:T(8,128)(2,1)} %bitcast.13, bf16[2,32,64,512]{3,2,1,0:T(8,128)(2,1)} %v_hbm.1, bf16[2,32,16,128]{3,2,1,0:T(8,128)(2,1)} %c_hbm.1, bf16[4096,128]{1,0:T(8,128)(2,1)} %bitcast.14, f32[2,32]{1,0:T(2,128)} %bitcast.15, f32[32,128]{1,0:T(8,128)} %cond_e.1, s32[1,256]{1,0:T(1,128)} %bitcast.16, ...), custom_call_target="tpu_custom_call" | custom-call | flops 2800000000 | bytes 8000000 | tf_op jit(solution)/shard_map/pallas_call | solution.py:441
  78.6 1.6 %copy.12 = f32[2,2,1,32,2,128]{5,4,3,2,1,0:T(2,128)} copy(f32[2,2,1,32,2,128]{5,4,3,2,1,0:T(2,128)} %bitcast.12) | data formatting | bytes 262144

commit v3 on v2

--- a/solution.py
+++ b/solution.py
@@ -27,7 +27,7 @@
     x_hbm, v_hbm, c_hbm, w_hbm, val_e, cond_e, grid_row, opp_row,
     out,
     x, v, c, c_both, w, w32, fwd, inv, spread, send1, recv1, send2, recv2, band, own_x,
-    send_y, recv_y, own_z, send_z, recv_z, total, peer_total, send_p, recv_p, full, mirror,
+    send_y, recv_y, own_z, send_z, recv_z, total, peer_total, send_p, recv_p, full, mirror, own_part,
     load_sem, self_sem, s0, r0, s1, r1, s2, r2, sy, ry, sz, rz, sp, rp, st, rt,
 ):
     m = lax.axis_index("mom")
@@ -140,17 +140,23 @@
                 send1[b, ch, :, :, 128 * q : 128 * (q + 1)] = (
                     spread[q, 256 * b : 256 * (b + 1), :].astype(BF16).reshape(16, 16, 128)
                 )
+        return carry
+
+    def pair_and_send(ch, carry):
+        pair_chunk(ch, carry)
         send_first(0, ch)
         return carry
 
     load_c.wait()
+    pair_chunk(0, 0)
     pl.semaphore_wait(barrier, len(peers))
+    send_first(0, 0)
     half = pl.ds(16 * (1 - pc), 16)
     points = pl.ds(aligned(16 * pc, 16), 16)
     points_other = pl.ds(aligned(16 * (1 - pc), 16), 16)
     share_c = remote(c.at[:, half], c_both.at[:, :, points], s0, r0, (m, p_other))
     share_c.start()
-    lax.fori_loop(0, 4, pair_chunk, 0)
+    lax.fori_loop(1, 4, pair_and_send, 0)
     c_both[:, :, points] = c[:, pl.ds(16 * pc, 16)]
 
     def make_tables():
@@ -360,6 +366,58 @@
             ).start()
         core_copy(b).start()
 
+    def y_sent(u):
+        for d in range(1, 4):
+            y_copy(u, d).wait_send()
+
+    def z_sent(u):
+        for d in range(1, 4):
+            z_copy(u, d).wait_send()
+
+    def swap_sent(b):
+        core_copy(b).wait_send()
+        for e in range(2):
+            swap_from(b, e).wait_send()
+
+    def place(b):
+        core_copy(b).wait_recv()
+        for e in range(2):
+            swap_from(b, e).wait_recv()
+        for ri in range(2):
+            for kk in range(2):
+                for row in range(2):
+                    part = slice(8 * row, 8 * row + 8)
+                    u = b * 2 + kk
+                    full[b, ri, row, pl.ds(aligned(16 * pc + 8 * kk, 8), 8), :] = total[u, ri, pc, part]
+                    full[b, ri, row, pl.ds(aligned(16 * (1 - pc) + 8 * kk, 8), 8), :] = peer_total[u, ri, part]
+                    for core in range(2):
+                        mirror[b, ri, row, 16 * core + 8 * kk : 16 * core + 8 * kk + 8, :] = recv_p[
+                            b, core, kk, ri
+                        ].astype(F32)[part]
+
+    def own_term():
+        for row in range(2):
+            energy = jnp.sum(jnp.where(slot == across, val_e[row : row + 1, :], 0.0), axis=1, keepdims=True)
+            gap = cond_e[...] - energy
+            for b in range(2):
+                for ri in range(2):
+                    rows = pl.ds((ri * 2 + b) * 512 + 2 * (p % 8) + row, 32, stride=16)
+                    result = gap * own_x[rows, :]
+                    own_part[b, ri, row] = -result if b else result
+
+    def add_mirrored(b):
+        for row in range(2):
+            for ri in range(2):
+                mirrored = dot(pick, mirror[b, ri, row].astype(BF16), TN)
+                here = full[b, ri, row]
+                down = mirrored if ri == 0 else -mirrored
+                own_part[1 - b, ri, row] += -down if b else down
+                own_part[b, ri, row] += here if b else -here
+
+    slot = lax.broadcasted_iota(jnp.int32, (32, 32), 0)
+    across = lax.broadcasted_iota(jnp.int32, (32, 32), 1)
+    pick = jnp.where(slot == (opp_row[...] & 31), 1.0, 0.0).astype(BF16)
+    own_term()
     second_arrived(0, 0)
     band_unit(0, 0)
     y_start(0)
@@ -380,55 +438,29 @@
     z_start(2)
     finish(1)
     swap_start(0)
+    second_sent(1, 0)
+    second_sent(1, 1)
+    for u in range(3):
+        y_sent(u)
+    z_sent(0)
+    z_sent(1)
     z_start(3)
     finish(2)
+    place(0)
+    add_mirrored(0)
+    y_sent(3)
     finish(3)
     swap_start(1)
-
-    slot = lax.broadcasted_iota(jnp.int32, (32, 32), 0)
-    pick = jnp.where(slot == (opp_row[...] & 31), 1.0, 0.0).astype(BF16)
-    across = lax.broadcasted_iota(jnp.int32, (32, 32), 1)
-    gaps = []
-    for row in range(2):
-        energy = jnp.sum(jnp.where(slot == across, val_e[row : row + 1, :], 0.0), axis=1, keepdims=True)
-        gaps.append(cond_e[...] - energy)
-    for b in range(2):
-        core_copy(b).wait_recv()
-        for e in range(2):
-            swap_from(b, e).wait_recv()
-        for ri in range(2):
-            for kk in range(2):
-                for row in range(2):
-                    part = slice(8 * row, 8 * row + 8)
-                    u = b * 2 + kk
-                    full[b, ri, row, pl.ds(aligned(16 * pc + 8 * kk, 8), 8), :] = total[u, ri, pc, part]
-                    full[b, ri, row, pl.ds(aligned(16 * (1 - pc) + 8 * kk, 8), 8), :] = peer_total[u, ri, part]
-                    for core in range(2):
-                        mirror[b, ri, row, 16 * core + 8 * kk : 16 * core + 8 * kk + 8, :] = recv_p[
-                            b, core, kk, ri
-                        ].astype(F32)[part]
+    z_sent(2)
+    z_sent(3)
+    swap_sent(0)
+    place(1)
+    add_mirrored(1)
     for row in range(2):
         for b in range(2):
             for ri in range(2):
-                own = own_x[pl.ds((ri * 2 + b) * 512 + 2 * (p % 8) + row, 32, stride=16), :]
-                mirrored = dot(pick, mirror[1 - b, ri, row].astype(BF16), TN)
-                here = full[b, ri, row]
-                turned = mirrored if ri == 0 else -mirrored
-                result = gaps[row] * own - here - turned
-                if b == 1:
-                    result = -gaps[row] * own + here + turned
-                out[pl.ds((ri * 2 + b) * 64 + row, 32, stride=2), :] = result
-
-    second_sent(1, 0)
-    second_sent(1, 1)
-    for u in range(4):
-        for d in range(1, 4):
-            y_copy(u, d).wait_send()
-            z_copy(u, d).wait_send()
-    for b in range(2):
-        core_copy(b).wait_send()
-        for e in range(2):
-            swap_from(b, e).wait_send()
+                out[pl.ds((ri * 2 + b) * 64 + row, 32, stride=2), :] = own_part[b, ri, row]
+    swap_sent(1)
 
 
 def on_device(
@@ -440,7 +472,7 @@
     dma = pltpu.SemaphoreType.DMA
     out = pl.pallas_call(
         kernel,
-        out_shape=jax.ShapeDtypeStruct((256, 128), F32),
+        out_shape=pltpu.VMEM((256, 128), F32),
         in_specs=[hbm] * 4 + [vmem] * 4,
         out_specs=vmem,
         scratch_shapes=[
@@ -470,6 +502,7 @@
             pltpu.VMEM((2, 2, 2, 2, 16, 128), BF16),
             pltpu.VMEM((2, 2, 2, 32, 128), F32),
             pltpu.VMEM((2, 2, 2, 32, 128), F32),
+            pltpu.VMEM((2, 2, 2, 32, 128), F32),
             dma((10,)), dma((12,)), dma, dma, dma((64,)), dma((64,)), dma((64,)), dma((64,)),
             dma((12,)), dma((12,)), dma((12,)), dma((12,)), dma((4,)), dma((4,)), dma((2,)), dma((2,)),
         ],

time: 80.3 us -> 77.3 us (0.963)
  Pallas kernels: 78.6 us -> 76.4 us
  local copies, waits for them, and re-layouts: 1.57 us -> 0.66 us
    pallas_call x1, Pallas kernels: 78.6 us -> 76.4 us  [on_device(): pl.pallas_call(kernel, out_shape=pltpu.VMEM((256, 128), F32), in_specs=[h...]
    unnamed x1, local copies, waits for them, and re-layouts: 1.57 us -> 0.66 us
where the time goes in v3:
time: 77.3 us; the launch traced here: 77.1 us
  Pallas kernels  76.4 us (99%)
    pallas_call x1, Pallas kernels, on_device(): pl.pallas_call(kernel, out_shape=pltpu.VMEM((256, 128), F32), in_specs=[h...  76.4 us

profile of v3, /device:TPU:1, one launch (start us, length us, event | category | flops | bytes accessed | tf_op | source)
XLA Modules:
  0.0 77.1 jit_solution(10986047424858972334)
XLA Ops:
  0.0 76.4 %shard_map.82 = f32[256,128]{1,0:T(8,128)S(1)} custom-call(bf16[2,2,32,64,128]{4,3,2,1,0:T(8,128)(2,1)} %bitcast.13, bf16[2,32,64,512]{3,2,1,0:T(8,128)(2,1)} %v_hbm.1, bf16[2,32,16,128]{3,2,1,0:T(8,128)(2,1)} %c_hbm.1, bf16[4096,128]{1,0:T(8,128)(2,1)} %bitcast.14, f32[2,32]{1,0:T(2,128)} %bitcast.15, f32[32,128]{1,0:T(8,128)} %cond_e.1, ...), custom_call_target="tpu_custom_call" | custom-call | flops 2800000000 | bytes 8000000 | tf_op jit(solution)/shard_map/pallas_call | solution.py:473
  76.5 0.7 copy.12

commit v4 on v3

v4 whole, which is shorter than its diff:
```python
import math

import jax
import jax.numpy as jnp
from jax import lax
from jax.experimental import pallas as pl
from jax.experimental.pallas import tpu as pltpu
from jax.sharding import PartitionSpec as P

MESH = pl.DeviceIdType.MESH
F32 = jnp.float32
BF16 = jnp.bfloat16
NT = (((1,), (1,)), ((), ()))
TN = (((0,), (0,)), ((), ()))
ORDER = (2, 6, 1, 5, 3, 7, 4)
WIDE = tuple((d, e, t) for d in (2, 1, 3, 0) for t in (1, 0) for e in (0, 1) if d + e + t)
UNITS = ((0, 0, 2), (0, 2, 2), (1, 0, 2), (1, 2, 1), (1, 3, 1))


def dot(a, b, dims=(((1,), (0,)), ((), ()))):
    return lax.dot_general(a, b, dims, preferred_element_type=F32)


def aligned(value, by):
    return pl.multiple_of(value, by)


def kernel(
    x_hbm, v_hbm, c_hbm, w_hbm, val_e, cond_e, grid_row, opp_row,
    out,
    x, v, c, c_both, w, w32, fwd, inv, spread, send1, recv1, send2, recv2, band, own_x,
    send_y, recv_y, own_z, send_z, recv_z, send_w, recv_w, total, peer_total,
    send_p, recv_p, mirror,
    load_sem, self_sem, s0, r0, s1, r1, s2, r2, sy, ry, sz, rz, sw, rw, sp, rp, st, rt,
):
    m = lax.axis_index("mom")
    p = lax.axis_index("pts")
    mx, mz = m % 4, m // 4
    py, ph, pc = p // 8, (p // 2) % 4, p % 2
    p_other = p + 1 - 2 * pc

    def mom_to(j):
        return ((mz + j // 4) % 2) * 4 + (mx + j % 4) % 4

    def mom_from(j):
        return ((mz + j // 4) % 2) * 4 + (mx + 4 - j % 4) % 4

    def pts_of(e):
        return p_other if e else p

    def core_of(e):
        return 1 - pc if e else pc

    def y_to(d):
        return (m, ((py + d) % 4) * 8 + p % 8)

    def z_to(d):
        return (m, py * 8 + ((ph + d) % 4) * 2 + pc)

    def wide_to(d, e, t):
        return ((m + 4 * t) % 8, py * 8 + ((ph + d) % 4) * 2 + core_of(e))

    def remote(src, dst, send, recv, peer):
        return pltpu.make_async_remote_copy(
            src_ref=src, dst_ref=dst, send_sem=send, recv_sem=recv, device_id=peer, device_id_type=MESH
        )

    def load_x(ch):
        rows = pl.ds(8 * ch, 8)
        return pltpu.make_async_copy(x_hbm.at[:, :, rows], x.at[:, :, rows], load_sem.at[ch])

    def load_v(ch):
        rows = pl.ds(8 * ch, 8)
        return pltpu.make_async_copy(v_hbm.at[:, rows], v.at[:, rows], load_sem.at[4 + ch])

    load_c = pltpu.make_async_copy(c_hbm, c, load_sem.at[8])
    load_w = pltpu.make_async_copy(w_hbm, w, load_sem.at[9])
    load_c.start()
    load_x(0).start()
    load_v(0).start()

    barrier = pltpu.get_barrier_semaphore()
    peers = [(mom_to(j), pts_of(e)) for j in range(8) for e in range(2) if j + e]
    peers += [y_to(d) for d in range(1, 4)] + [wide_to(d, e, t) for d, e, t in WIDE if d]
    for peer in peers:
        pl.semaphore_signal(barrier, inc=1, device_id=peer, device_id_type=MESH)

    lane = lax.broadcasted_iota(jnp.int32, (32, 128), 1)
    sign = jnp.where(lane < 64, -1.0, 1.0).astype(F32)

    def first_copy(b, ch, j, src_m, dst_m, peer):
        i = (b * 4 + ch) * 8 + j
        return remote(
            send1.at[b, ch, pl.ds(2 * dst_m, 2)],
            recv1.at[b, :, pl.ds(aligned((src_m * 4 + ch) * 16, 16), 16), :],
            s1.at[i],
            r1.at[i],
            (peer, p),
        )

    def first_self(b, ch):
        return pltpu.make_async_copy(
            send1.at[b, ch, pl.ds(2 * m, 2)],
            recv1.at[b, :, pl.ds(aligned((m * 4 + ch) * 16, 16), 16), :],
            self_sem.at[b * 4 + ch],
        )

    def send_first(b, ch):
        for j in ORDER:
            first_copy(b, ch, j, m, mom_to(j), mom_to(j)).start()
        first_self(b, ch).start()

    def pair_chunk(ch):
        for group in range(2):
            ks = [group * 4 + u for u in range(4)]
            halves = []
            for k8 in ks:
                k = ch * 8 + k8
                xk = jnp.concatenate([x[0, 0, k], x[1, 0, k], x[0, 1, k], x[1, 1, k]], axis=0)
                ck = jnp.concatenate([c[0, k], c[1, k]], axis=0)
                halves.append(dot(ck, xk, NT))
            lefts = []
            for h in halves:
                parts = []
                for b in range(2):
                    cols = h[:, 128 * b : 128 * (b + 1)]
                    q = cols[:16] + sign[:16] * pltpu.roll(cols[16:], 64, 1)
                    parts += [q, pltpu.roll(q, 64, 1) * -sign[:16]]
                lefts.append(jnp.concatenate(parts, axis=0).astype(BF16))
            for k8, left in zip(ks, lefts):
                k = ch * 8 + k8
                pair = dot(left, jnp.concatenate([v[0, k], v[1, k]], axis=0))
                for b in range(2):
                    for ri in range(2):
                        top = (b * 2 + ri) * 16
                        for q in range(4):
                            spread.at[q][pl.ds(b * 256 + ri * 8 + k8, 16, stride=16), :] = pair[
                                top : top + 16, 128 * q : 128 * (q + 1)
                            ]

    def pack(b, ch):
        for q in range(4):
            send1[b, ch, :, :, 128 * q : 128 * (q + 1)] = (
                spread[q, 256 * b : 256 * (b + 1), :].astype(BF16).reshape(16, 16, 128)
            )

    def pair_and_send(ch, carry):
        load_x(ch).wait()
        load_v(ch).wait()
        pair_chunk(ch)
        pack(0, ch)
        send_first(0, ch)
        pack(1, ch)
        return carry

    load_c.wait()
    load_x(0).wait()
    load_v(0).wait()
    for ch in range(1, 4):
        load_x(ch).start()
        load_v(ch).start()
    load_w.start()
    pair_chunk(0)
    pack(0, 0)
    pl.semaphore_wait(barrier, len(peers))
    send_first(0, 0)
    pack(1, 0)
    half = pl.ds(16 * (1 - pc), 16)
    points = pl.ds(aligned(16 * pc, 16), 16)
    points_other = pl.ds(aligned(16 * (1 - pc), 16), 16)
    share_c = remote(c.at[:, half], c_both.at[:, :, points], s0, r0, (m, p_other))
    share_c.start()
    lax.fori_loop(1, 4, pair_and_send, 0)
    c_both[:, :, points] = c[:, pl.ds(16 * pc, 16)]

    def make_tables():
        frequency = lax.broadcasted_iota(jnp.int32, (256, 256), 0)
        angle = ((frequency * grid_row[...]) & 255).astype(F32) * (2.0 * math.pi / 256)
        slot = lax.broadcasted_iota(jnp.int32, (256, 512), 0)
        column = lax.broadcasted_iota(jnp.int32, (256, 512), 1)
        cos_table = jnp.cos(angle).astype(BF16)
        sin_table = jnp.sin(angle).astype(BF16)

        def halves(slots, real):
            place = jnp.where(slot == slots, 1.0, 0.0).astype(BF16)
            cosine, sine = dot(cos_table, place), dot(sin_table, place)
            return jnp.where(real, cosine, sine), jnp.where(real, -sine, cosine)

        top, bottom = halves((column >> 4) * 8 + (column & 7), (column & 8) == 0)
        fwd[:256, :] = top.astype(BF16)
        fwd[256:, :] = bottom.astype(BF16)
        top, bottom = halves((column >> 5) * 16 + ((column >> 3) & 3) * 4 + (column & 3), (column & 4) == 0)
        inv[:, :256] = (top.T * (1.0 / 256)).astype(BF16)
        inv[:, 256:] = (bottom.T * (1.0 / 256)).astype(BF16)

    make_tables()
    first_row = aligned((p // 8) * 16, 16)
    for ri in range(2):
        for b in range(2):
            piece = x[ri, b, :, pl.ds(first_row, 16), :].astype(F32)
            own_x[pl.ds((ri * 2 + b) * 512, 512), :] = piece.reshape(512, 128)
    load_w.wait()
    w32[...] = w[...].astype(F32)

    def second_copy(u, j, e, src_m, src_c, dst_m, dst_c, peer):
        b, q, n = UNITS[u]
        i = (u * 8 + j) * 2 + e
        return remote(
            send2.at[b, dst_m * 2 + dst_c, pl.ds(q, n)],
            recv2.at[b, pl.ds(q, n), src_c * 8 + src_m],
            s2.at[i],
            r2.at[i],
            peer,
        )

    def second_to(u, j, e):
        return second_copy(u, j, e, m, pc, mom_to(j), core_of(e), (mom_to(j), pts_of(e)))

    def second_from(u, j, e):
        return second_copy(u, j, e, mom_from(j), core_of(e), m, pc, (mom_to(j), pts_of(e)))

    def second_self(u):
        b, q, n = UNITS[u]
        return pltpu.make_async_copy(
            send2.at[b, m * 2 + pc, pl.ds(q, n)], recv2.at[b, pl.ds(q, n), pc * 8 + m], self_sem.at[8 + u]
        )

    def send_second(u):
        for j in ORDER + (0,):
            for e in range(2):
                if j + e:
                    second_to(u, j, e).start()
        second_self(u).start()

    def second_sent(u):
        for j in ORDER + (0,):
            for e in range(2):
                if j + e:
                    second_to(u, j, e).wait_send()

    def first_sent(b, ch):
        for j in ORDER:
            first_copy(b, ch, j, m, mom_to(j), mom_to(j)).wait_send()

    def first_arrived(b):
        def step(ch, carry):
            for j in range(1, 8):
                first_copy(b, ch, j, mom_from(j), m, mom_to(j)).wait_recv()
            first_self(b, ch).wait()
            return carry

        lax.fori_loop(0, 4, step, 0)

    def transform_block(b):
        for nu in range(2):

            def transform(half, carry, nu=nu):
                cols = pl.ds(aligned(half * 256, 256), 256)
                spec = dot(fwd[...], recv1[b, nu, :, cols])
                real, imag = spec[:256], spec[256:]

                def weight(ri):
                    return jnp.concatenate(
                        [w32[pl.ds(ri * 2048 + (2 * half + t) * 2 + nu, 256, stride=8), :] for t in range(2)],
                        axis=1,
                    )

                wr, wi = weight(0), weight(1)
                prod = jnp.concatenate([wr * real - wi * imag, wr * imag + wi * real], axis=0)
                back = dot(inv[...], prod.astype(BF16)).reshape(16, 4, 8, 256)
                send2[b, :, :, 8 * nu : 8 * nu + 8, cols] = back.astype(BF16)
                return carry

            lax.fori_loop(0, 2, transform, 0)

    def resend(ch, carry):
        first_sent(0, ch)
        send_first(1, ch)
        return carry

    lax.fori_loop(0, 4, resend, 0)
    first_arrived(0)
    transform_block(0)
    first_sent(1, 0)
    first_sent(1, 1)
    send_second(0)
    first_sent(1, 2)
    first_sent(1, 3)
    send_second(1)
    first_arrived(1)
    transform_block(1)
    second_sent(0)
    send_second(2)
    share_c.wait_send()
    remote(c.at[:, half], c_both.at[:, :, points_other], s0, r0, (m, p_other)).wait_recv()

    def second_arrived(u):
        for j in range(8):
            for e in range(2):
                if j + e:
                    second_from(u, j, e).wait_recv()
        second_self(u).wait()

    def momenta(u):
        return 4 * UNITS[u][2]

    def band_unit(u):
        b, first, n = UNITS[u]
        for i in range(n):
            for t in range(4):
                spread[t, 256 * i : 256 * (i + 1), :] = (
                    recv2[b, first + i, :, :, 128 * t : 128 * (t + 1)].astype(F32).reshape(256, 128)
                )
        mixed = []
        for i in range(4 * n):
            rows = [
                jnp.concatenate(
                    [
                        spread.at[t][pl.ds((i // 4) * 256 + ri * 4 + i % 4, 32, stride=8), :]
                        for t in range(4)
                    ],
                    axis=1,
                )
                for ri in range(2)
            ]
            k = 16 * pc + 4 * first + i
            vk = jnp.concatenate([v[0, k], v[1, k]], axis=0)
            mixed.append(dot(jnp.concatenate(rows, axis=0).astype(BF16), vk, NT))
        lefts = []
        for o in mixed:
            q = o[:32] + sign * pltpu.roll(o[32:], 64, 1)
            lefts.append(jnp.concatenate([q, pltpu.roll(q, 64, 1) * -sign], axis=0).astype(BF16))
        for i, left in enumerate(lefts):
            ck = jnp.concatenate([c_both[0, 4 * first + i], c_both[1, 4 * first + i]], axis=0)
            band[u][pl.ds(i, 128, stride=4 * n), :] = dot(left, ck, TN)

    def y_copy(u, d):
        i = u * 3 + d - 1
        return remote(send_y[u].at[d - 1], recv_y[u].at[d - 1], sy.at[i], ry.at[i], y_to(d))

    def z_copy(u, d):
        i = u * 3 + d - 1
        return remote(send_z[u].at[d - 1], recv_z[u].at[d - 1], sz.at[i], rz.at[i], z_to(d))

    def y_start(u):
        k = momenta(u)
        for d in (2, 1, 3):
            for ri in range(2):
                row = aligned((ri * 4 + (py + d) % 4) * 16 * k, 16 * k)
                send_y[u][d - 1, ri] = band[u][pl.ds(row, 16 * k), :].astype(BF16)
            y_copy(u, d).start()

    def z_start(u):
        k = momenta(u)
        for d in range(1, 4):
            y_copy(u, d).wait_recv()
        for d in (2, 1, 3, 0):
            zz = aligned(((ph + d) % 4) * 4 * k, 4 * k)
            for ri in range(2):
                part = band[u][pl.ds(aligned((ri * 4 + py) * 16 * k + zz, 4 * k), 4 * k), :]
                for i in range(3):
                    part += recv_y[u][i, ri, pl.ds(zz, 4 * k), :].astype(F32)
                if d == 0:
                    own_z[u][ri] = part
                else:
                    send_z[u][d - 1, ri] = part.astype(BF16)
            if d:
                z_copy(u, d).start()

    def swap_to(u, e):
        i = u * 2 + e
        return remote(send_p[u].at[e], recv_p[u].at[pc], sp.at[i], rp.at[i], ((m + 4) % 8, pts_of(e)))

    def swap_from(u, e):
        i = u * 2 + e
        return remote(send_p[u].at[e], recv_p[u].at[core_of(e)], sp.at[i], rp.at[i], ((m + 4) % 8, pts_of(e)))

    def core_copy(u):
        return remote(total[u].at[:, 1 - pc], peer_total[u], st.at[u], rt.at[u], (m, p_other))

    def finish(u):
        k = momenta(u)
        for d in range(1, 4):
            z_copy(u, d).wait_recv()
        for ri in range(2):
            part = own_z[u][ri]
            for i in range(3):
                part += recv_z[u][i, ri].astype(F32)
            total[u][ri] = part.reshape(2, 2 * k, 128)
        swap_start(u)

    def wide_copy(u, d, e, t, source):
        i = ((u - 3) * 2 + t) * 8 + e * 4 + d
        return remote(
            send_w.at[u - 3, d, core_of(e)], recv_w.at[u - 3, t, source, d], sw.at[i], rw.at[i], wide_to(d, e, t)
        )

    def wide_start(u):
        for d in range(1, 4):
            y_copy(u, d).wait_recv()
        for d in (2, 1, 3, 0):
            zz = aligned(((ph + d) % 4) * 16, 16)
            for ri in range(2):
                part = band[u][pl.ds(aligned((ri * 4 + py) * 64 + zz, 16), 16), :]
                for i in range(3):
                    part += recv_y[u][i, ri, pl.ds(zz, 16), :].astype(F32)
                if d == 0:
                    total[u][ri] = part.reshape(2, 8, 128)
                for core in range(2):
                    send_w[u - 3, d, core, 8 * ri : 8 * ri + 8, :] = part[8 * core : 8 * core + 8].astype(BF16)
            for dd, e, t in WIDE:
                if dd == d:
                    wide_copy(u, d, e, t, pc).start()
        recv_w[u - 3, 0, pc, 0] = jnp.zeros((16, 128), BF16)

    def wide_place(u):
        b, first, _ = UNITS[u]
        for d, e, t in WIDE:
            wide_copy(u, d, e, t, core_of(e)).wait_recv()
        for core in range(2):
            here, there = [sum(recv_w[u - 3, t, core, d].astype(F32) for d in range(4)) for t in range(2)]
            for ri in range(2):
                for row in range(2):
                    part = slice(8 * ri + 4 * row, 8 * ri + 4 * row + 4)
                    top = 16 * core + 4 * first
                    mirror[b, ri, row, top : top + 4, :] = there[part]
                    rows = out_rows(b, ri, row, top, 4)
                    before = out[rows, :]
                    out[rows, :] = before + here[part] if b else before - here[part]
        for ri in range(2):
            own = total[u][ri, pc]
            for row in range(2):
                part = own[4 * row : 4 * row + 4]
                rows = out_rows(b, ri, row, 16 * pc + 4 * first, 4)
                before = out[rows, :]
                out[rows, :] = before + part if b else before - part

    def swap_start(u):
        k = momenta(u)
        for e in range(2):
            for ri in range(2):
                send_p[u][e, 2 * k * ri : 2 * k * (ri + 1), :] = total[u][ri, core_of(e)].astype(BF16)
            swap_to(u, e).start()
        core_copy(u).start()

    def y_sent(u):
        for d in range(1, 4):
            y_copy(u, d).wait_send()

    def z_sent(u):
        for d in range(1, 4):
            z_copy(u, d).wait_send()

    def swap_sent(u):
        core_copy(u).wait_send()
        for e in range(2):
            swap_to(u, e).wait_send()

    def out_rows(b, ri, row, first, count):
        return pl.ds((ri * 2 + b) * 64 + row + 2 * first, count, stride=2)

    def own_term():
        for row in range(2):
            energy = jnp.sum(jnp.where(slot == across, val_e[row : row + 1, :], 0.0), axis=1, keepdims=True)
            gap = cond_e[...] - energy
            for b in range(2):
                for ri in range(2):
                    rows = pl.ds((ri * 2 + b) * 512 + 2 * (p % 8) + row, 32, stride=16)
                    result = gap * own_x[rows, :]
                    out[out_rows(b, ri, row, 0, 32), :] = -result if b else result

    def place(u):
        b, first, n = UNITS[u]
        k = 4 * n
        for e in range(2):
            swap_from(u, e).wait_recv()
        for core in range(2):
            turned = recv_p[u][core].astype(F32)
            for ri in range(2):
                for row in range(2):
                    top = (2 * ri + row) * k
                    mirror[b, ri, row, 16 * core + 4 * first : 16 * core + 4 * first + k, :] = turned[top : top + k]
        core_copy(u).wait_recv()
        for ri in range(2):
            for row in range(2):
                for e in range(2):
                    part = peer_total[u][ri] if e else total[u][ri, pc]
                    part = part[k * row : k * (row + 1)]
                    rows = out_rows(b, ri, row, 16 * core_of(e) + 4 * first, k)
                    before = out[rows, :]
                    out[rows, :] = before + part if b else before - part

    def add_mirrored(b):
        for row in range(2):
            for ri in range(2):
                mirrored = dot(pick, mirror[b, ri, row].astype(BF16), TN)
                rows = out_rows(1 - b, ri, row, 0, 32)
                before = out[rows, :]
                out[rows, :] = before - mirrored if b != ri else before + mirrored

    slot = lax.broadcasted_iota(jnp.int32, (32, 32), 0)
    across = lax.broadcasted_iota(jnp.int32, (32, 32), 1)
    pick = jnp.where(slot == (opp_row[...] & 31), 1.0, 0.0).astype(BF16)
    own_term()
    second_arrived(0)
    band_unit(0)
    y_start(0)
    second_sent(1)
    send_second(3)
    second_arrived(1)
    band_unit(1)
    y_start(1)
    z_start(0)
    second_sent(2)
    send_second(4)
    second_arrived(2)
    band_unit(2)
    y_start(2)
    z_start(1)
    finish(0)
    second_arrived(3)
    band_unit(3)
    y_start(3)
    z_start(2)
    finish(1)
    second_arrived(4)
    band_unit(4)
    y_start(4)
    wide_start(3)
    finish(2)
    place(0)
    place(1)
    wide_start(4)
    add_mirrored(0)
    second_sent(3)
    second_sent(4)
    place(2)
    for u in range(5):
        y_sent(u)
    for u in range(3):
        z_sent(u)
        swap_sent(u)
    wide_place(3)
    wide_place(4)
    add_mirrored(1)
    for u in (3, 4):
        for d, e, t in WIDE:
            wide_copy(u, d, e, t, pc).wait_send()


def on_device(
    amplitudes, val_orbitals, cond_orbitals, screened, val_energy, cond_energy, grid_of_slot, opposite_slot
):
    weights = screened.reshape(2, 256, 2, 4, 128).transpose(0, 1, 3, 2, 4).reshape(4096, 128)
    hbm = pl.BlockSpec(memory_space=pl.ANY)
    vmem = pl.BlockSpec(memory_space=pltpu.VMEM)
    dma = pltpu.SemaphoreType.DMA

    def each(shape):
        return tuple(shape(4 * n) for _, _, n in UNITS)

    out = pl.pallas_call(
        kernel,
        out_shape=pltpu.VMEM((256, 128), F32),
        in_specs=[hbm] * 4 + [vmem] * 4,
        out_specs=vmem,
        scratch_shapes=[
            pltpu.VMEM((2, 2, 32, 64, 128), BF16),
            pltpu.VMEM((2, 32, 64, 512), BF16),
            pltpu.VMEM((2, 32, 16, 128), BF16),
            pltpu.VMEM((2, 16, 32, 128), BF16),
            pltpu.VMEM((4096, 128), BF16),
            pltpu.VMEM((4096, 128), F32),
            pltpu.VMEM((512, 512), BF16),
            pltpu.VMEM((512, 512), BF16),
            pltpu.VMEM((4, 512, 128), F32),
            pltpu.VMEM((2, 4, 16, 16, 512), BF16),
            pltpu.VMEM((2, 2, 512, 512), BF16),
            pltpu.VMEM((2, 16, 4, 16, 512), BF16),
            pltpu.VMEM((2, 4, 16, 16, 512), BF16),
            each(lambda k: pltpu.VMEM((128 * k, 128), F32)),
            pltpu.VMEM((2048, 128), F32),
            each(lambda k: pltpu.VMEM((3, 2, 16 * k, 128), BF16)),
            each(lambda k: pltpu.VMEM((3, 2, 16 * k, 128), BF16)),
            each(lambda k: pltpu.VMEM((2, 4 * k, 128), F32)),
            each(lambda k: pltpu.VMEM((3, 2, 4 * k, 128), BF16)),
            each(lambda k: pltpu.VMEM((3, 2, 4 * k, 128), BF16)),
            pltpu.VMEM((2, 4, 2, 16, 128), BF16),
            pltpu.VMEM((2, 2, 2, 4, 16, 128), BF16),
            each(lambda k: pltpu.VMEM((2, 2, 2 * k, 128), F32)),
            each(lambda k: pltpu.VMEM((2, 2 * k, 128), F32)),
            each(lambda k: pltpu.VMEM((2, 4 * k, 128), BF16)),
            each(lambda k: pltpu.VMEM((2, 4 * k, 128), BF16)),
            pltpu.VMEM((2, 2, 2, 32, 128), F32),
            dma((10,)), dma((13,)), dma, dma, dma((64,)), dma((64,)), dma((80,)), dma((80,)),
            dma((15,)), dma((15,)), dma((15,)), dma((15,)), dma((32,)), dma((32,)), dma((10,)), dma((10,)), dma((5,)), dma((5,)),
        ],
        compiler_params=pltpu.CompilerParams(
            collective_id=0, has_side_effects=True, vmem_limit_bytes=56 * 2**20
        ),
        cost_estimate=pl.CostEstimate(flops=2800000000, bytes_accessed=8000000, transcendentals=131072),
    )(
        amplitudes.reshape(2, 2, 32, 64, 128),
        val_orbitals,
        cond_orbitals,
        weights,
        val_energy.T,
        cond_energy,
        grid_of_slot.reshape(1, 256),
        opposite_slot.reshape(1, 32),
    )
    return out.reshape(2, 2, 1, 32, 2, 128)


def solution(mesh):
    in_specs = (
        P(None, None, None, "mom", None, None),
        P(None, "mom", None, None),
        P(None, "mom", "pts", None),
        P(None, None, ("pts", "mom"), None),
        P("mom", "pts"),
        P("mom", None),
        P(),
        P("mom"),
    )
    out_specs = P(None, None, None, "mom", "pts", None)
    return jax.shard_map(
        on_device, mesh=mesh, in_specs=in_specs, out_specs=out_specs, check_vma=False
    )
```

time: 77.3 us -> 76.3 us (0.987)
  Pallas kernels: 76.4 us -> 75.5 us
    pallas_call x1, Pallas kernels: 76.4 us -> 75.5 us  [on_device(): pl.pallas_call(kernel, out_shape=pltpu.VMEM((256, 128), F32), in_specs=[h...]
where the time goes in v4:
time: 76.3 us; the launch traced here: 76.2 us
  Pallas kernels  75.5 us (99%)
    pallas_call x1, Pallas kernels, on_device(): pl.pallas_call(kernel, out_shape=pltpu.VMEM((256, 128), F32), in_specs=[h...  75.5 us

profile of v4, /device:TPU:1, one launch (start us, length us, event | category | flops | bytes accessed | tf_op | source)
XLA Modules:
  0.0 76.2 jit_solution(13576421495052432622)
XLA Ops:
  0.0 75.5 %shard_map.82 = f32[256,128]{1,0:T(8,128)S(1)} custom-call(bf16[2,2,32,64,128]{4,3,2,1,0:T(8,128)(2,1)} %bitcast.13, bf16[2,32,64,512]{3,2,1,0:T(8,128)(2,1)} %v_hbm.1, bf16[2,32,16,128]{3,2,1,0:T(8,128)(2,1)} %c_hbm.1, bf16[4096,128]{1,0:T(8,128)(2,1)} %bitcast.14, f32[2,32]{1,0:T(2,128)} %bitcast.15, f32[32,128]{1,0:T(8,128)} %cond_e.1, ...), custom_call_target="tpu_custom_call" | custom-call | flops 2800000000 | bytes 8000000 | tf_op jit(solution)/shard_map/pallas_call | solution.py:562
  75.5 0.7 copy.12

commit v5 on v4

--- a/solution.py
+++ b/solution.py
@@ -338,9 +338,41 @@
         i = u * 3 + d - 1
         return remote(send_y[u].at[d - 1], recv_y[u].at[d - 1], sy.at[i], ry.at[i], y_to(d))
 
+    way = 1 - 2 * pc
+
+    def z_place(steps):
+        return (ph + way * steps + 8) % 4
+
     def z_copy(u, d):
         i = u * 3 + d - 1
-        return remote(send_z[u].at[d - 1], recv_z[u].at[d - 1], sz.at[i], rz.at[i], z_to(d))
+        peer = z_to(d)
+        if u < 2:
+            peer = (m, py * 8 + z_place(-1 if d == 2 else 1) * 2 + pc)
+        return remote(send_z[u].at[d - 1], recv_z[u].at[d - 1], sz.at[i], rz.at[i], peer)
+
+    def z_part(u, ri, place):
+        k = momenta(u)
+        zz = aligned(place * 4 * k, 4 * k)
+        part = band[u][pl.ds(aligned((ri * 4 + py) * 16 * k + zz, 4 * k), 4 * k), :]
+        for i in range(3):
+            part += recv_y[u][i, ri, pl.ds(zz, 4 * k), :].astype(F32)
+        return part
+
+    def relay_start(u):
+        for d in range(1, 4):
+            y_copy(u, d).wait_recv()
+        for d, steps in ((1, 2), (2, -1)):
+            for ri in range(2):
+                send_z[u][d - 1, ri] = z_part(u, ri, z_place(steps)).astype(BF16)
+            z_copy(u, d).start()
+        for ri in range(2):
+            own_z[u][ri] = z_part(u, ri, ph)
+
+    def relay_pass(u):
+        z_copy(u, 1).wait_recv()
+        for ri in range(2):
+            send_z[u][2, ri] = (z_part(u, ri, z_place(1)) + recv_z[u][0, ri].astype(F32)).astype(BF16)
+        z_copy(u, 3).start()
 
     def y_start(u):
         k = momenta(u)
@@ -380,11 +412,12 @@
 
     def finish(u):
         k = momenta(u)
-        for d in range(1, 4):
-            z_copy(u, d).wait_recv()
+        slots = (1, 2) if u < 2 else (0, 1, 2)
+        for i in slots:
+            z_copy(u, i + 1).wait_recv()
         for ri in range(2):
             part = own_z[u][ri]
-            for i in range(3):
+            for i in slots:
                 part += recv_z[u][i, ri].astype(F32)
             total[u][ri] = part.reshape(2, 2 * k, 128)
         swap_start(u)
@@ -510,27 +543,29 @@
     second_arrived(1)
     band_unit(1)
     y_start(1)
-    z_start(0)
+    relay_start(0)
     second_sent(2)
     send_second(4)
     second_arrived(2)
     band_unit(2)
     y_start(2)
-    z_start(1)
-    finish(0)
+    relay_start(1)
+    relay_pass(0)
     second_arrived(3)
     band_unit(3)
     y_start(3)
     z_start(2)
-    finish(1)
+    finish(0)
+    relay_pass(1)
     second_arrived(4)
     band_unit(4)
     y_start(4)
     wide_start(3)
+    finish(1)
     finish(2)
     place(0)
+    wide_start(4)
     place(1)
-    wide_start(4)
     add_mirrored(0)
     second_sent(3)
     second_sent(4)

time: 76.3 us -> 75.9 us (level)
  no operation moved by 1% of the time
where the time goes in v5:
time: 75.9 us; the launch traced here: 75.7 us
  Pallas kernels  75.1 us (99%)
    pallas_call x1, Pallas kernels, on_device(): pl.pallas_call(kernel, out_shape=pltpu.VMEM((256, 128), F32), in_specs=[h...  75.1 us

profile of v5, /device:TPU:1, one launch (start us, length us, event | category | flops | bytes accessed | tf_op | source)
XLA Modules:
  0.0 75.7 jit_solution(16882128547673370698)
XLA Ops:
  0.0 75.1 %shard_map.82 = f32[256,128]{1,0:T(8,128)S(1)} custom-call(bf16[2,2,32,64,128]{4,3,2,1,0:T(8,128)(2,1)} %bitcast.13, bf16[2,32,64,512]{3,2,1,0:T(8,128)(2,1)} %v_hbm.1, bf16[2,32,16,128]{3,2,1,0:T(8,128)(2,1)} %c_hbm.1, bf16[4096,128]{1,0:T(8,128)(2,1)} %bitcast.14, f32[2,32]{1,0:T(2,128)} %bitcast.15, f32[32,128]{1,0:T(8,128)} %cond_e.1, ...), custom_call_target="tpu_custom_call" | custom-call | flops 2800000000 | bytes 8000000 | tf_op jit(solution)/shard_map/pallas_call | solution.py:597
  75.1 0.7 copy.12
